TPU v7x, 256 devices: a whole 4x4x8 slice. The times are simulated.
256 devices in a mesh: section: 8 (over z_lo, core), dom: 32 (over y, z_hi, x).
Axes of the slice: x: 4, y: 4, z: 8 (z_hi: 2, z_lo: 4; z = z_hi * 4 + z_lo), core: 2. Of those that a mesh axis runs over, the one named last changes fastest.
Arguments:
- blocks: float32 [64, 64, 6, 128, 128], P('section', 'dom'), may hold values from -0.21875 to 0.21875
- column_index: int32 [64, 64, 6], P('section', 'dom'), may hold values from 0 to 63
- block_period: int32 [64, 64, 6], P('section', 'dom'), may hold values from 0 to 63, as said below
- cost_vector: float32 [64, 8192], P('section', 'dom'), may hold values from -6 to 6
- demand: float32 [64, 8192], P('section', 'dom'), may hold values from -12 to 12
- primal_start: float32 [64, 8192], P('section', 'dom'), may hold values from 0 to 2
- dual_start: float32 [64, 8192], P('section', 'dom'), may hold values from -3 to 3
- primal_weight: float32 [1], replicated, may hold values from 0.5 to 2
Outputs:
- primal_final: float32 [64, 8192], P('section', 'dom')
- dual_final: float32 [64, 8192], P('section', 'dom')
Inputs may be any that keep to these rules, and one draw needn't show every extreme that they name: block_period[p, r, k] is p or p - 1; it is p for k = 0 and for p = 0.
All inputs are finite; a program needn't handle non-finite values.
Results may differ from a plain program's by a relative error of at most 0.00011.
Values sent between devices are 32-bit elements; how exact they have to be, the bound alone decides.
No kernel may reach another device: no remote copies, remote signals or barrier semaphores. Data moves between devices by JAX's collectives and lax.ppermute only.
A program may use at most 64 MiB of HBM per device.

v0:
```python
import functools

import jax
import jax.numpy as jnp
from jax import lax
from jax.sharding import Mesh
from jax.sharding import PartitionSpec as P

SECTION = ("section_0", "section_1")
DOM = ("dom_0", "dom_1", "dom_2")
SECTION_DOM = ("section_0", "section_1", "dom_0", "dom_1", "dom_2")


step_scale = 0.4
epsilon = 1e-06


def copy_for_each(x, axis):
    copies = jnp.broadcast_to(x, (lax.axis_size(axis), *x.shape))
    return lax.all_to_all(copies, axis, split_axis=0, concat_axis=0, tiled=True)


def in_order(pieces, dim):
    pieces = jnp.moveaxis(pieces, 0, dim)
    shape = pieces.shape
    return pieces.reshape(*shape[:dim], shape[dim] * shape[dim + 1], *shape[dim + 2 :])


def collect(x, axis, dim):
    pieces = copy_for_each(x, axis)
    return in_order(pieces, dim)


def passed_along(block, axis, distance):
    devices = range(lax.axis_size(axis))
    route = [(i - distance, i) for i in devices if i - distance in devices]
    return lax.ppermute(block, axis, route)


def cut_along(x, dim, count):
    before, after = (x.shape[:dim], x.shape[dim + 1 :])
    return jnp.moveaxis(x.reshape(*before, count, -1, *after), dim, 0)


def summed_on_arrival(x, axis, dim):
    pieces = cut_along(x, dim, lax.axis_size(axis))
    arrived = lax.all_to_all(pieces, axis, split_axis=0, concat_axis=0, tiled=True)
    return arrived.sum(axis=0)


def by_axis(x, axes):
    return functools.reduce(lax.psum, axes, x)


def slot_layout(column_index, block_period):
    periods_here = column_index.shape[0]
    local_period = jnp.arange(periods_here, dtype=jnp.int32)[:, None, None]
    global_period = lax.axis_index(SECTION) * periods_here + local_period
    slot_index = local_period + block_period - global_period + 1
    return slot_index


def forward(blocks, column_index, slot_index, field):
    periods_here = field.shape[0]
    width_here = blocks.shape[-1]
    gathered = collect(field, DOM, 1)
    carried = passed_along(gathered[-1:], SECTION, 1)
    stacked = jnp.concatenate([carried, gathered], axis=0)
    block_count = stacked.shape[1] // width_here
    picked = stacked.reshape(periods_here + 1, block_count, width_here)[slot_index, column_index]
    product = jnp.einsum("prkij,prkj->pri", blocks, picked, precision=lax.Precision.HIGHEST)
    return product.reshape(periods_here, -1)


def adjoint(blocks, column_index, slot_index, field):
    periods_here = field.shape[0]
    rows_here = blocks.shape[1]
    width_here = blocks.shape[-1]
    block_count = rows_here * lax.axis_size(DOM)
    field_blocks = field.reshape(periods_here, rows_here, width_here)
    block_terms = jnp.einsum(
        "prkij,pri->prkj", blocks, field_blocks, precision=lax.Precision.HIGHEST
    )
    segment_ids = (slot_index * block_count + column_index).reshape(-1)
    dense_term = jax.ops.segment_sum(
        block_terms.reshape(-1, width_here),
        segment_ids,
        num_segments=(periods_here + 1) * block_count,
    )
    dense_term = dense_term.reshape(periods_here + 1, block_count * width_here)
    carried = passed_along(dense_term[:1], SECTION, -1)
    own_rows = dense_term[1:]
    merged = own_rows + jnp.concatenate([jnp.zeros_like(own_rows[:-1]), carried], axis=0)
    result = summed_on_arrival(merged, DOM, 1)
    return result


def on_device(
    blocks, column_index, block_period, cost_vector, demand, primal_start, dual_start, primal_weight
):
    slot_index = slot_layout(column_index, block_period)
    weight_now = primal_weight[0]
    tau_first = step_scale / weight_now
    sigma_first = step_scale * weight_now
    primal_one = jnp.maximum(
        0.0,
        primal_start
        - tau_first * (cost_vector - adjoint(blocks, column_index, slot_index, dual_start)),
    )
    dual_one = dual_start + sigma_first * (
        demand - forward(blocks, column_index, slot_index, 2.0 * primal_one - primal_start)
    )
    local_primal = jnp.sum((primal_one - primal_start) ** 2)
    local_dual = jnp.sum((dual_one - dual_start) ** 2)
    move_primal, move_dual = (by_axis(local_primal, SECTION_DOM), by_axis(local_dual, SECTION_DOM))
    weight_next = jnp.sqrt(weight_now * jnp.sqrt((move_dual + epsilon) / (move_primal + epsilon)))
    tau_second = step_scale / weight_next
    sigma_second = step_scale * weight_next
    primal_final = jnp.maximum(
        0.0,
        primal_one
        - tau_second * (cost_vector - adjoint(blocks, column_index, slot_index, dual_one)),
    )
    dual_final = dual_one + sigma_second * (
        demand - forward(blocks, column_index, slot_index, 2.0 * primal_final - primal_one)
    )
    return (primal_final, dual_final)


def solution(mesh):
    finer = Mesh(
        mesh.devices.reshape(4, 2, 4, 2, 4), ("section_0", "section_1", "dom_0", "dom_1", "dom_2")
    )
    return jax.shard_map(
        on_device,
        mesh=finer,
        in_specs=(
            P(SECTION, DOM, None, None, None),
            P(SECTION, DOM, None),
            P(SECTION, DOM, None),
            P(SECTION, DOM),
            P(SECTION, DOM),
            P(SECTION, DOM),
            P(SECTION, DOM),
            P(),
        ),
        out_specs=(P(SECTION, DOM), P(SECTION, DOM)),
        check_vma=False,
    )
```

profile of v0, /device:TPU:1, one launch (start us, length us, event | category | flops | bytes accessed | tf_op | source)
XLA Modules:
  0.0 172.5 jit_solution(11084496139171217123)
XLA Ops:
  0.6 0.0 copy-start.1
  0.6 0.0 copy-start.2
  0.7 0.7 fusion.14
  1.4 0.1 copy.18
  1.5 0.1 reshape.73
  1.6 6.1 %fusion.10 = f32[8,2,1,6,128]{4,2,3,1,0:T(1,128)S(1)} fusion(f32[8,2,6,128,128]{4,3,2,1,0:T(8,128)} %param.8, f32[8,2,128,1,1]{2,0,1,3,4:T(8,128)} %bitcast.64), kind=kOutput, calls=%fused_computation.24 | convolution fusion | flops 18874368 | bytes 6348800 | tf_op jit(solution)/shard_map/prkij,pri->prkj/dot_general | solution.py:81
  7.7 1.0 scatter_custom_fusion
  8.7 5.1 %collective-permute-start = (f32[1,8192]{1,0:T(1,128)S(1)}, f32[1,8192]{1,0:T(1,128)S(1)}, u32[]{:S(2)}, u32[]{:S(2)}) collective-permute-start(f32[1,8192]{1,0:T(1,128)S(1)} %bitcast.69), channel_id=1, source_target_pairs={{32,0},{64,32},{96,64},{128,96},{160,128},{192,160},{224,192},{33,... | collective-permute-start | bytes 98312 | tf_op jit(solution)/shard_map/ppermute | solution.py:37
  13.9 0.1 slice.37
  14.0 1.3 collective-permute-done
  15.3 0.7 pad_add_fusion.1
  16.0 13.2 %all-to-all-start = ((f32[32,8,256]{2,1,0:T(8,128)}), f32[32,8,256]{2,1,0:T(8,128)S(1)}, u32[]{:S(2)}, u32[]{:S(2)}) async-start(f32[32,8,256]{2,1,0:T(8,128)} %bitcast.6), calls=%async_computation | async-start | bytes 524288 | tf_op jit(solution)/shard_map/all_to_all | solution.py:47
  29.9 12.1 %all-to-all-done = f32[32,8,256]{2,1,0:T(8,128)S(1)} async-done(((f32[32,8,256]{2,1,0:T(8,128)}), f32[32,8,256]{2,1,0:T(8,128)S(1)}, u32[]{:S(2)}, u32[]{:S(2)}) %all-to-all-start) | async-done | bytes 262176 | tf_op jit(solution)/shard_map/all_to_all | solution.py:47
  42.0 0.0 copy-done.1
  42.0 0.0 copy-done.2
  42.0 0.6 multiply_reduce_fusion
  42.7 15.2 %all_to_all.20 = f32[32,8,256]{2,1,0:T(8,128)S(1)} all-to-all(f32[32,8,256]{2,1,0:T(8,128)S(1)} %broadcast_in_dim.15), channel_id=1, replica_groups=mesh['section_0'=4,'section_1'=2,'dom_0'=4,'dom_1'=2,'dom_2'=4] {'dom_0'..., dimensions={0} | all-to-all | bytes 524288 | tf_op jit(solution)/shard_map/all_to_all | solution.py:20
  57.9 7.8 %collective-permute-start.1 = (f32[1,8192]{1,0:T(1,128)S(1)}, f32[1,8192]{1,0:T(1,128)S(1)}, u32[]{:S(2)}, u32[]{:S(2)}) collective-permute-start(f32[1,8192]{1,0:T(1,128)S(1)} %bitcast.67), channel_id=1, source_target_pairs={{0,32},{32,64},{64,96},{96,128},{128,160},{160,192},{192,224},{1,3... | collective-permute-start | bytes 98312 | tf_op jit(solution)/shard_map/ppermute | solution.py:37
  65.7 0.1 copy.20
  65.8 0.1 reshape.59
  65.9 0.1 copy.19
  66.0 0.7 collective-permute-done.1
  66.7 1.4 gather_fusion
  68.1 7.1 %fusion.18 = f32[8,2,1,128,1]{3,2,4,1,0:T(1,128)S(1)} fusion(f32[8,2,6,128,1]{3,4,2,1,0:T(1,128)S(1)} %bitcast.60, f32[8,2,6,128,128]{4,3,2,1,0:T(8,128)} %param.8), kind=kOutput, calls=%fused_computation.40 | convolution fusion | flops 18874368 | bytes 6348800 | tf_op jit(solution)/shard_map/prkij,prkj->pri/dot_general | solution.py:71
  75.2 0.0 copy-done
  75.2 0.0 copy-done.3
  75.2 0.7 multiply_reduce_fusion.1
  75.9 5.1 %fusion.8 = f32[8,2,1,6,128]{4,2,3,1,0:T(1,128)S(1)} fusion(f32[8,2,6,128,128]{4,3,2,1,0:T(8,128)} %param.8, f32[8,2,128,1,1]{2,0,1,3,4:T(8,128)S(1)} %bitcast.63), kind=kOutput, calls=%fused_computation.22 | convolution fusion | flops 18874368 | bytes 6348800 | tf_op jit(solution)/shard_map/prkij,pri->prkj/dot_general | solution.py:81
  81.0 1.0 scatter_custom_fusion.1
  82.0 1.9 %collective-permute-start.2 = (f32[1,8192]{1,0:T(1,128)S(1)}, f32[1,8192]{1,0:T(1,128)S(1)}, u32[]{:S(2)}, u32[]{:S(2)}) collective-permute-start(f32[1,8192]{1,0:T(1,128)S(1)} %bitcast.70), channel_id=1, source_target_pairs={{32,0},{64,32},{96,64},{128,96},{160,128},{192,160},{224,192},{33,... | collective-permute-start | bytes 98312 | tf_op jit(solution)/shard_map/ppermute | solution.py:37
  83.9 0.1 slice.43
  84.0 3.8 %collective-permute-done.2 = f32[1,8192]{1,0:T(1,128)S(1)} collective-permute-done((f32[1,8192]{1,0:T(1,128)S(1)}, f32[1,8192]{1,0:T(1,128)S(1)}, u32[]{:S(2)}, u32[]{:S(2)}) %collective-permute-start.2) | collective-permute-done | bytes 32800 | tf_op jit(solution)/shard_map/ppermute | solution.py:37
  87.8 0.7 pad_add_fusion
  88.5 3.9 %all-to-all-start.2 = ((f32[32,8,256]{2,1,0:T(8,128)}), f32[32,8,256]{2,1,0:T(8,128)S(1)}, u32[]{:S(2)}, u32[]{:S(2)}) async-start(f32[32,8,256]{2,1,0:T(8,128)} %bitcast.18), calls=%async_computation.2 | async-start | bytes 524288 | tf_op jit(solution)/shard_map/all_to_all | solution.py:47
  92.4 9.6 %all-reduce.4 = (f32[]{:T(128)}, f32[]{:T(128)}) all-reduce(f32[]{:T(128)} %get-tuple-element.16, f32[]{:T(128)} %get-tuple-element.14), channel_id=1, replica_groups=mesh['section_0'=4,'section_1'=2,'dom_0'=4,'dom_1'=2,'dom_2'=4] {'sectio..., use_global_device_ids=true, to_apply=%region_3.0 | all-reduce | flops 2 | bytes 16 | tf_op jit(solution)/shard_map/psum | solution.py:52
  102.0 4.1 %all-reduce.6 = (f32[]{:T(128)}, f32[]{:T(128)}) all-reduce(f32[]{:T(128)} %get-tuple-element.6, f32[]{:T(128)} %get-tuple-element.7), channel_id=1, replica_groups=mesh['section_0'=4,'section_1'=2,'dom_0'=4,'dom_1'=2,'dom_2'=4] {'sectio..., use_global_device_ids=true, to_apply=%region_4.0 | all-reduce | flops 2 | bytes 16 | tf_op jit(solution)/shard_map/psum | solution.py:52
  106.1 9.5 %all-reduce.3 = (f32[]{:T(128)}, f32[]{:T(128)}) all-reduce(f32[]{:T(128)} %get-tuple-element.10, f32[]{:T(128)} %get-tuple-element.11), channel_id=1, replica_groups=mesh['section_0'=4,'section_1'=2,'dom_0'=4,'dom_1'=2,'dom_2'=4] {'dom_0'}, use_global_device_ids=true, to_apply=%region_5.0 | all-reduce | flops 2 | bytes 16 | tf_op jit(solution)/shard_map/psum | solution.py:52
  115.6 8.4 %all-reduce.5 = (f32[]{:T(128)}, f32[]{:T(128)}) all-reduce(f32[]{:T(128)} %get-tuple-element.4, f32[]{:T(128)} %get-tuple-element.5), channel_id=1, replica_groups=mesh['section_0'=4,'section_1'=2,'dom_0'=4,'dom_1'=2,'dom_2'=4] {'dom_1'}, use_global_device_ids=true, to_apply=%region_6.0 | all-reduce | flops 2 | bytes 16 | tf_op jit(solution)/shard_map/psum | solution.py:52
  124.0 9.0 %all-reduce.2 = (f32[]{:T(128)}, f32[]{:T(128)}) all-reduce(f32[]{:T(128)} %get-tuple-element.8, f32[]{:T(128)} %get-tuple-element.9), channel_id=1, replica_groups=mesh['section_0'=4,'section_1'=2,'dom_0'=4,'dom_1'=2,'dom_2'=4] {'dom_2'}, use_global_device_ids=true, to_apply=%region_7.0 | all-reduce | flops 2 | bytes 16 | tf_op jit(solution)/shard_map/psum | solution.py:52
  134.4 0.0 all-to-all-done.2
  134.5 0.6 multiply_subtract_fusion
  135.1 18.7 %all_to_all.21 = f32[32,8,256]{2,1,0:T(8,128)S(1)} all-to-all(f32[32,8,256]{2,1,0:T(8,128)S(1)} %broadcast_in_dim.18), channel_id=1, replica_groups=mesh['section_0'=4,'section_1'=2,'dom_0'=4,'dom_1'=2,'dom_2'=4] {'dom_0'..., dimensions={0} | all-to-all | bytes 524288 | tf_op jit(solution)/shard_map/all_to_all | solution.py:20
  153.9 8.7 %collective-permute-start.3 = (f32[1,8192]{1,0:T(1,128)S(1)}, f32[1,8192]{1,0:T(1,128)S(1)}, u32[]{:S(2)}, u32[]{:S(2)}) collective-permute-start(f32[1,8192]{1,0:T(1,128)S(1)} %bitcast.68), channel_id=1, source_target_pairs={{0,32},{32,64},{64,96},{96,128},{128,160},{160,192},{192,224},{1,3... | collective-permute-start | bytes 98312 | tf_op jit(solution)/shard_map/ppermute | solution.py:37
  162.6 0.1 copy.21
  162.7 0.7 collective-permute-done.3
  163.4 1.4 gather_fusion.1
  164.8 7.1 %fusion.19 = f32[8,2,1,128,1]{3,2,4,1,0:T(1,128)S(1)} fusion(f32[8,2,6,128,1]{3,4,2,1,0:T(1,128)S(1)} %bitcast.59, f32[8,2,6,128,128]{4,3,2,1,0:T(8,128)} %param.8), kind=kOutput, calls=%fused_computation.41 | convolution fusion | flops 18874368 | bytes 6348800 | tf_op jit(solution)/shard_map/prkij,prkj->pri/dot_general | solution.py:71
  171.9 0.6 fusion.5
  (22 shorter events, 0.3 us)
Async XLA Ops:
  0.6 41.4 %copy-start.1 = (f32[8,256]{1,0:T(8,128)S(1)}, f32[8,256]{1,0:T(8,128)}, u32[]{:S(2)}) copy-start(f32[8,256]{1,0:T(8,128)} %param.13) | copy-start | bytes 24580
  0.6 41.4 %copy-start.2 = (f32[8,256]{1,0:T(8,128)S(1)}, f32[8,256]{1,0:T(8,128)}, u32[]{:S(2)}) copy-start(f32[8,256]{1,0:T(8,128)} %param.11) | copy-start | bytes 24580
  7.7 67.5 %copy-start = (f32[8,256]{1,0:T(8,128)S(1)}, f32[8,256]{1,0:T(8,128)}, u32[]{:S(2)}) copy-start(f32[8,256]{1,0:T(8,128)} %param.14) | copy-start | bytes 24580
  7.7 67.5 %copy-start.3 = (f32[8,256]{1,0:T(8,128)S(1)}, f32[8,256]{1,0:T(8,128)}, u32[]{:S(2)}) copy-start(f32[8,256]{1,0:T(8,128)} %param.12) | copy-start | bytes 24580
  8.7 6.5 %collective-permute-start = (f32[1,8192]{1,0:T(1,128)S(1)}, f32[1,8192]{1,0:T(1,128)S(1)}, u32[]{:S(2)}, u32[]{:S(2)}) collective-permute-start(f32[1,8192]{1,0:T(1,128)S(1)} %bitcast.69), channel_id=1, source_target_pairs={{32,0},{64,32},{96,64},{128,96},{160,128},{192,160},{224,192},{33,... | collective-permute-start | bytes 98312 | tf_op jit(solution)/shard_map/ppermute | solution.py:37
  16.0 26.0 %all-to-all-start = ((f32[32,8,256]{2,1,0:T(8,128)}), f32[32,8,256]{2,1,0:T(8,128)S(1)}, u32[]{:S(2)}, u32[]{:S(2)}) async-start(f32[32,8,256]{2,1,0:T(8,128)} %bitcast.6), calls=%async_computation | async-start | bytes 524288 | tf_op jit(solution)/shard_map/all_to_all | solution.py:47
  57.9 8.8 %collective-permute-start.1 = (f32[1,8192]{1,0:T(1,128)S(1)}, f32[1,8192]{1,0:T(1,128)S(1)}, u32[]{:S(2)}, u32[]{:S(2)}) collective-permute-start(f32[1,8192]{1,0:T(1,128)S(1)} %bitcast.67), channel_id=1, source_target_pairs={{0,32},{32,64},{64,96},{96,128},{128,160},{160,192},{192,224},{1,3... | collective-permute-start | bytes 98312 | tf_op jit(solution)/shard_map/ppermute | solution.py:37
  82.0 5.8 %collective-permute-start.2 = (f32[1,8192]{1,0:T(1,128)S(1)}, f32[1,8192]{1,0:T(1,128)S(1)}, u32[]{:S(2)}, u32[]{:S(2)}) collective-permute-start(f32[1,8192]{1,0:T(1,128)S(1)} %bitcast.70), channel_id=1, source_target_pairs={{32,0},{64,32},{96,64},{128,96},{160,128},{192,160},{224,192},{33,... | collective-permute-start | bytes 98312 | tf_op jit(solution)/shard_map/ppermute | solution.py:37
  88.5 45.9 %all-to-all-start.2 = ((f32[32,8,256]{2,1,0:T(8,128)}), f32[32,8,256]{2,1,0:T(8,128)S(1)}, u32[]{:S(2)}, u32[]{:S(2)}) async-start(f32[32,8,256]{2,1,0:T(8,128)} %bitcast.18), calls=%async_computation.2 | async-start | bytes 524288 | tf_op jit(solution)/shard_map/all_to_all | solution.py:47
  153.9 9.5 %collective-permute-start.3 = (f32[1,8192]{1,0:T(1,128)S(1)}, f32[1,8192]{1,0:T(1,128)S(1)}, u32[]{:S(2)}, u32[]{:S(2)}) collective-permute-start(f32[1,8192]{1,0:T(1,128)S(1)} %bitcast.68), channel_id=1, source_target_pairs={{0,32},{32,64},{64,96},{96,128},{128,160},{160,192},{192,224},{1,3... | collective-permute-start | bytes 98312 | tf_op jit(solution)/shard_map/ppermute | solution.py:37
where the time goes:
time: 173 us
  blocking collectives  74.5 us (43%)
  starting transfers between devices  40.6 us (23%)
  matrix products  25.4 us (15%)
  waiting for transfers between devices  18.6 us (11%)
  other arithmetic  6.8 us (4%)
  local copies, waits for them, and re-layouts  3.65 us (2%)
  between operations  3.07 us (2%)
    psum x5, blocking collectives, by_axis(): return functools.reduce(lax.psum, axes, x)  40.6 us
    all_to_all x2, blocking collectives, copy_for_each(): return lax.all_to_all(copies, axis, split_axis=0, concat_axis=0, tiled=True)  33.9 us
    ppermute x4, starting transfers between devices, passed_along(): return lax.ppermute(block, axis, route)  23.5 us
    all_to_all x2, starting transfers between devices, summed_on_arrival(): lax.all_to_all(pieces, axis, split_axis=0, concat_axis=0, tiled=True)  17.1 us
    dot_general x2, matrix products, forward(): jnp.einsum('prkij,prkj->pri', blocks, picked, precision=lax.Precision.HIG...  14.2 us
    all_to_all x2, waiting for transfers between devices, summed_on_arrival(): lax.all_to_all(pieces, axis, split_axis=0, concat_axis=0, tiled=True)  12.1 us
    dot_general x2, matrix products, adjoint(): jnp.einsum('prkij,pri->prkj', blocks, field_blocks, precision=lax.Precisi...  11.2 us
    ppermute x4, waiting for transfers between devices, passed_along(): return lax.ppermute(block, axis, route)  6.48 us
  transfers between devices with their start and end apart: 6, of which 5 were waited for; matrix products, arithmetic and copies ran while one was open for 0% of the time, Pallas kernels for 0%

commit v1 on v0

v1 whole, which is shorter than its diff:
```python
import functools

import jax
import jax.numpy as jnp
from jax import lax
from jax.experimental import pallas as pl
from jax.experimental.pallas import tpu as pltpu
from jax.sharding import Mesh
from jax.sharding import PartitionSpec as P

AXES = ("section_0", "section_1", "dom_0", "dom_1", "dom_2")
SECTION = ("section_0", "section_1")
DOM = ("dom_0", "dom_1", "dom_2")
PLANE = ("dom_0", "dom_2")
TWIN = "dom_1"

step_scale = 0.4
epsilon = 1e-06

PEERS = 16
PERIODS_HERE = 8
LATER = tuple(range(1, 8))
CHUNK = 32
PIECE = 40

f32 = jnp.float32
VMEM = pl.BlockSpec(memory_space=pltpu.VMEM)
SMEM = pl.BlockSpec(memory_space=pltpu.SMEM)
PARAMS = pltpu.CompilerParams(vmem_limit_bytes=32 << 20)


def shaped(*shape):
    return jax.ShapeDtypeStruct(shape, f32)


def call(kernel, outs, ins, scratch=(), alias={}):
    return pl.pallas_call(
        kernel,
        out_shape=outs,
        in_specs=ins,
        out_specs=jax.tree.map(lambda _: VMEM, outs),
        scratch_shapes=list(scratch),
        input_output_aliases=alias,
        compiler_params=PARAMS,
    )


def columns_of(ref):
    rows = jnp.concatenate([ref[:, :128], ref[:, 128:], jnp.zeros((112, 128), f32)], axis=0)
    return rows.T


def store_rows(ref, rows):
    ref[:, :128] = rows[0:8]
    ref[:, 128:] = rows[8:16]


def transposed_product(block, wide):
    return jnp.sum(block * wide, axis=0, keepdims=True)


def partial_row(row):
    return row + (row >> 5) * 8


def slot(t, r, k):
    return t * 12 + r * 6 + k


def add_terms(blocks_ref, index_ref, dest_ref, t, r, wide, spread):
    for k in range(6):
        row = index_ref[slot(t, r, k)]
        if spread:
            row = partial_row(row)
        dest_ref[pl.ds(row, 1), :] += transposed_product(blocks_ref[t, r, k], wide)


def row_product(blocks_ref, index_ref, source_ref, t, r):
    total = jnp.zeros((128, 128), f32)
    for k in range(6):
        total += blocks_ref[t, r, k] * source_ref[pl.ds(index_ref[slot(t, r, k)], 1), :]
    return jnp.sum(total, axis=1, keepdims=True)


def adjoint_first(index_ref, blocks_ref, dual_ref, own_ref, carry_ref, terms):
    terms[...] = jnp.zeros_like(terms)
    columns = columns_of(dual_ref)
    for r in range(2):
        wide = jnp.broadcast_to(columns[:, r * 8 : r * 8 + 1], (128, 128))
        add_terms(blocks_ref, index_ref, terms, 0, r, wide, False)
    own_ref[...] = terms[0:64]
    carry_ref[...] = terms[64:128]


def adjoint_later(index_ref, blocks_ref, dual_ref, own_ref, partial_ref):
    partial_ref[...] = jnp.zeros_like(partial_ref)
    for p in range(PEERS):
        partial_ref[pl.ds(p * PIECE, 4, stride=8), :] = own_ref[p * 4 : p * 4 + 4]
    columns = columns_of(dual_ref)
    for t in LATER:
        for r in range(2):
            place = r * 8 + t
            wide = jnp.broadcast_to(columns[:, place : place + 1], (128, 128))
            add_terms(blocks_ref, index_ref, partial_ref, t, r, wide, True)


def add_carried(partial_in, carried_ref, partial_ref):
    for p in range(PEERS):
        rows = pl.ds(p * PIECE + 7, 4, stride=8)
        partial_ref[rows, :] = partial_in[rows, :] + carried_ref[p * 4 : p * 4 + 4]


def add_own_and_carried(partial_in, own_ref, carried_ref, move_x, move_a, move_b, partial_ref):
    for p in range(PEERS):
        rows = pl.ds(p * PIECE, 4, stride=8)
        partial_ref[rows, :] = partial_in[rows, :] + own_ref[p * 4 : p * 4 + 4]
        rows = pl.ds(p * PIECE + 7, 4, stride=8)
        partial_ref[rows, :] = partial_in[rows, :] + carried_ref[p * 4 : p * 4 + 4]
    tile = jnp.concatenate([move_x[...], move_a[...] + move_b[...], jnp.zeros((6, 128), f32)], 0)
    for p in range(PEERS):
        partial_ref[p * PIECE + CHUNK : (p + 1) * PIECE, :] = tile


def total_of(pieces_ref):
    total = pieces_ref[0]
    for p in range(1, PEERS):
        total = total + pieces_ref[p]
    return total


def sum_and_pack(pieces_ref, primal_ref, cost_ref, pack_ref):
    pack_ref[0:CHUNK, :] = total_of(pieces_ref)[0:CHUNK]
    pack_ref[32:40, :] = primal_ref[:, :128]
    pack_ref[40:48, :] = primal_ref[:, 128:]
    pack_ref[48:56, :] = cost_ref[:, :128]
    pack_ref[56:64, :] = cost_ref[:, 128:]


def sum_only(pieces_ref, sum_ref):
    sum_ref[...] = total_of(pieces_ref)


def both_twins(own, other):
    first = lax.axis_index(TWIN) == 0
    return jnp.concatenate(
        [jnp.where(first, own, other), jnp.where(first, other, own)], axis=0
    )


def to_all(ref, value):
    for p in range(PEERS):
        ref[p] = value


def primal_step(weight_ref, pack_ref, other_ref, copies_ref, primal_one_ref, cost_ref, move_ref):
    tau = step_scale / jnp.full((CHUNK, 128), weight_ref[0], f32)
    product = pack_ref[0:32] + other_ref[0:32]
    start = both_twins(pack_ref[32:48], other_ref[32:48])
    cost = both_twins(pack_ref[48:64], other_ref[48:64])
    primal_one = jnp.maximum(0.0, start - tau * (cost - product))
    primal_one_ref[...] = primal_one
    cost_ref[...] = cost
    move_ref[...] = 0.5 * jnp.sum((primal_one - start) ** 2, axis=0, keepdims=True)
    to_all(copies_ref, 2.0 * primal_one - start)


def dual_later(
    index_ref, weight_ref, blocks_ref, field_ref, dual_ref, demand_ref, dual_one_ref, partial_ref, move_ref
):
    partial_ref[...] = jnp.zeros_like(partial_ref)
    sigma = step_scale * weight_ref[0]
    start = columns_of(dual_ref)
    demand = columns_of(demand_ref)
    lane = lax.broadcasted_iota(jnp.int32, (128, 128), 1)
    result = start
    for t in LATER:
        for r in range(2):
            place = r * 8 + t
            here = slice(place, place + 1)
            product = row_product(blocks_ref, index_ref, field_ref, t, r)
            dual_one = start[:, here] + sigma * (demand[:, here] - product)
            wide = jnp.broadcast_to(dual_one, (128, 128))
            result = jnp.where(lane == place, wide, result)
            add_terms(blocks_ref, index_ref, partial_ref, t, r, wide, True)
    move_ref[...] = jnp.sum((result - start).T ** 2, axis=0, keepdims=True)
    store_rows(dual_one_ref, result.T)


def first_rows(field_ref, carried_ref, rows):
    rows[0:64, :] = field_ref[pl.ds(0, 64, stride=8), :]
    rows[64:128, :] = carried_ref[...]


def dual_first(
    index_ref, weight_ref, blocks_ref, field_ref, carried_ref, dual_ref, demand_ref, later_ref,
    dual_one_ref, own_ref, carry_ref, move_ref, rows, terms,
):
    first_rows(field_ref, carried_ref, rows)
    terms[...] = jnp.zeros_like(terms)
    sigma = step_scale * weight_ref[0]
    start = columns_of(dual_ref)
    demand = columns_of(demand_ref)
    later = columns_of(later_ref)
    lane = lax.broadcasted_iota(jnp.int32, (128, 128), 1)
    result = start
    for r in range(2):
        here = slice(r * 8, r * 8 + 1)
        product = row_product(blocks_ref, index_ref, rows, 0, r)
        dual_one = start[:, here] + sigma * (demand[:, here] - product)
        wide = jnp.broadcast_to(dual_one, (128, 128))
        result = jnp.where(lane == r * 8, wide, result)
        later = jnp.where(lane == r * 8, wide, later)
        add_terms(blocks_ref, index_ref, terms, 0, r, wide, False)
    move_ref[...] = jnp.sum((result - start).T ** 2, axis=0, keepdims=True)
    store_rows(dual_one_ref, later.T)
    own_ref[...] = terms[0:64]
    carry_ref[...] = terms[64:128]


def spread_moves(sum_ref, other_ref, copies_ref):
    tile = sum_ref[CHUNK:PIECE] + other_ref[CHUNK:PIECE]
    for s in range(8):
        copies_ref[s] = tile


def primal_last(
    weight_ref, moves_ref, sum_ref, other_ref, primal_one_ref, cost_ref, copies_ref, primal_ref, steps_ref
):
    tile = moves_ref[0]
    for s in range(1, 8):
        tile = tile + moves_ref[s]
    move = jnp.broadcast_to(jnp.sum(tile, axis=1, keepdims=True), (8, 128))
    move_primal, move_dual = move[0:1], move[1:2]
    weight = jnp.full((1, 128), weight_ref[0], f32)
    omega = jnp.sqrt(weight * jnp.sqrt((move_dual + epsilon) / (move_primal + epsilon)))
    tau = step_scale / omega
    steps_ref[...] = jnp.broadcast_to(step_scale * omega, (8, 128))
    product = sum_ref[0:CHUNK] + other_ref[0:CHUNK]
    primal_one = primal_one_ref[...]
    primal = jnp.maximum(0.0, primal_one - tau * (cost_ref[...] - product))
    to_all(copies_ref, 2.0 * primal - primal_one)
    first = lax.axis_index(TWIN) == 0
    primal_ref[:, :128] = jnp.where(first, primal[0:8], primal[16:24])
    primal_ref[:, 128:] = jnp.where(first, primal[8:16], primal[24:32])


def last_later(index_ref, blocks_ref, field_ref, product_ref):
    lane = lax.broadcasted_iota(jnp.int32, (128, 128), 1)
    result = jnp.zeros((128, 128), f32)
    for t in LATER:
        for r in range(2):
            product = row_product(blocks_ref, index_ref, field_ref, t, r)
            result = jnp.where(lane == r * 8 + t, jnp.broadcast_to(product, (128, 128)), result)
    product_ref[...] = result


def last_first(
    index_ref, blocks_ref, field_ref, carried_ref, steps_ref, product_ref, dual_ref, demand_ref, out_ref, rows
):
    first_rows(field_ref, carried_ref, rows)
    lane = lax.broadcasted_iota(jnp.int32, (128, 128), 1)
    result = product_ref[...]
    for r in range(2):
        product = row_product(blocks_ref, index_ref, rows, 0, r)
        result = jnp.where(lane == r * 8, jnp.broadcast_to(product, (128, 128)), result)
    result = result.T
    sigma = steps_ref[...]
    for r in range(2):
        part = slice(r * 128, r * 128 + 128)
        out_ref[:, part] = dual_ref[:, part] + sigma * (
            demand_ref[:, part] - result[r * 8 : r * 8 + 8]
        )


def to_next(x, distance):
    route = [(i - distance, i) for i in range(8) if 0 <= i - distance < 8]
    return lax.ppermute(x, SECTION, route)


def to_twin(x):
    return lax.ppermute(x, TWIN, [(0, 1), (1, 0)])


def exchange(pieces, axis):
    return lax.all_to_all(pieces, axis, split_axis=0, concat_axis=0, tiled=True)


def block_rows(column_index, block_period):
    t = lax.broadcasted_iota(jnp.int32, column_index.shape, 0)
    period = lax.axis_index(SECTION) * PERIODS_HERE + t
    before = period - block_period
    c = column_index
    place = ((c >> 4) * 4 + ((c >> 1) & 3)) * 4 + ((c >> 3) & 1) * 2 + (c & 1)
    row = jnp.where(t == 0, place + 64 * before, place * 8 + t - before)
    return row.reshape(-1)


def on_device(
    blocks, column_index, block_period, cost_vector, demand, primal_start, dual_start, primal_weight
):
    index = block_rows(column_index, block_period)
    terms = pltpu.VMEM((128, 128), f32)
    half = shaped(64, 128)
    line = shaped(1, 128)
    partials = shaped(PEERS * PIECE, 128)
    chunk = shaped(CHUNK, 128)
    copies = shaped(PEERS, CHUNK, 128)
    local = shaped(8, 256)

    own, carry = call(adjoint_first, [half, half], [SMEM, VMEM, VMEM], [terms])(
        index, blocks, dual_start
    )
    carried = to_next(carry, -1)
    partial = call(adjoint_later, partials, [SMEM, VMEM, VMEM, VMEM])(index, blocks, dual_start, own)
    partial = call(add_carried, partials, [VMEM, VMEM], alias={0: 0})(partial, carried)
    pieces = exchange(partial.reshape(PEERS, PIECE, 128), PLANE)
    pack = call(sum_and_pack, shaped(64, 128), [VMEM] * 3)(pieces, primal_start, cost_vector)
    other = to_twin(pack)
    send, primal_one, cost, move_primal = call(
        primal_step, [copies, chunk, chunk, line], [SMEM, VMEM, VMEM]
    )(primal_weight, pack, other)
    field = exchange(send, PLANE).reshape(PEERS * CHUNK, 128)
    carried = to_next(field.reshape(64, 8, 128)[:, 7], 1)
    dual_some, partial, move_a = call(
        dual_later, [local, partials, line], [SMEM, SMEM] + [VMEM] * 4
    )(index, primal_weight, blocks, field, dual_start, demand)
    dual_one, own, carry, move_b = call(
        dual_first, [local, half, half, line], [SMEM, SMEM] + [VMEM] * 6, [terms, terms]
    )(index, primal_weight, blocks, field, carried, dual_start, demand, dual_some)
    carried = to_next(carry, -1)
    partial = call(add_own_and_carried, partials, [VMEM] * 6, alias={0: 0})(
        partial, own, carried, move_primal, move_a, move_b
    )
    pieces = exchange(partial.reshape(PEERS, PIECE, 128), PLANE)
    total = call(sum_only, shaped(PIECE, 128), [VMEM])(pieces)
    other = to_twin(total)
    moves = call(spread_moves, shaped(8, 8, 128), [VMEM] * 2)(total, other)
    moves = exchange(moves, SECTION)
    send, primal_final, steps = call(
        primal_last, [copies, local, shaped(8, 128)], [SMEM] + [VMEM] * 5
    )(primal_weight, moves, total, other, primal_one, cost)
    field = exchange(send, PLANE).reshape(PEERS * CHUNK, 128)
    carried = to_next(field.reshape(64, 8, 128)[:, 7], 1)
    product = call(last_later, shaped(128, 128), [SMEM, VMEM, VMEM])(index, blocks, field)
    dual_final = call(last_first, local, [SMEM] + [VMEM] * 7, [terms])(
        index, blocks, field, carried, steps, product, dual_one, demand
    )
    return primal_final, dual_final


def solution(mesh):
    finer = Mesh(mesh.devices.reshape(4, 2, 4, 2, 4), AXES)
    return jax.shard_map(
        on_device,
        mesh=finer,
        in_specs=(
            P(SECTION, DOM, None, None, None),
            P(SECTION, DOM, None),
            P(SECTION, DOM, None),
            P(SECTION, DOM),
            P(SECTION, DOM),
            P(SECTION, DOM),
            P(SECTION, DOM),
            P(),
        ),
        out_specs=(P(SECTION, DOM), P(SECTION, DOM)),
        check_vma=False,
    )
```

time: 173 us -> 108 us (0.62)
  matrix products: 25.4 us -> 0 us
  blocking collectives: 74.5 us -> 56.5 us
  waiting for transfers between devices: 18.6 us -> 5.78 us
  starting transfers between devices: 40.6 us -> 30.3 us
  Pallas kernels: 0 us -> 8.6 us
  other arithmetic: 6.8 us -> 0.74 us
    psum x5 -> x0, blocking collectives: 40.6 us -> none  [by_axis(): return functools.reduce(lax.psum, axes, x)]
    dot_general x4 -> x0, matrix products: 25.4 us -> none  [the longest x2 14.2 us: forward(): jnp.einsum('prkij,prkj->pri', blocks, picked, precision=lax.Precision.HIG...]
    all_to_all x2 -> x5, blocking collectives: 33.9 us -> 56.5 us  [exchange(): return lax.all_to_all(pieces, axis, split_axis=0, concat_axis=0, tiled=True)]
    all_to_all x2 -> x0, starting transfers between devices: 17.1 us -> none  [summed_on_arrival(): lax.all_to_all(pieces, axis, split_axis=0, concat_axis=0, tiled=True)]
    all_to_all x2 -> x0, waiting for transfers between devices: 12.1 us -> none  [summed_on_arrival(): lax.all_to_all(pieces, axis, split_axis=0, concat_axis=0, tiled=True)]
    pallas_call x0 -> x13, Pallas kernels: none -> 8.6 us  [the longest x1 2.57 us: on_device(): call(dual_later, [local, partials, line], [SMEM, SMEM] + [VMEM] * 4)]
    ppermute x4 -> x6, starting transfers between devices: 23.5 us -> 30.3 us  [the longest x4 17.7 us: to_next(): return lax.ppermute(x, SECTION, route)]
    unnamed x8 -> x14, local copies, waits for them, and re-layouts: 0.02 us -> 3.5 us
  transfers between devices with their start and end apart: 6 -> 6, of which waited for: 5 -> 4; matrix products, arithmetic and copies ran while one was open for 0% -> 0% of each run, Pallas kernels for 0% -> 4%
where the time goes in v1:
time: 108 us; the launch traced here: 107 us
  blocking collectives  56.5 us (52%)
  starting transfers between devices  30.3 us (28%)
  Pallas kernels  8.6 us (8%)
  waiting for transfers between devices  5.78 us (5%)
  local copies, waits for them, and re-layouts  3.75 us (3%)
  between operations  1.45 us (1%)
    all_to_all x5, blocking collectives, exchange(): return lax.all_to_all(pieces, axis, split_axis=0, concat_axis=0, tiled=True)  56.5 us
    ppermute x4, starting transfers between devices, to_next(): return lax.ppermute(x, SECTION, route)  17.7 us
    ppermute x2, starting transfers between devices, to_twin(): return lax.ppermute(x, TWIN, [(0, 1), (1, 0)])  12.6 us
    ppermute x4, waiting for transfers between devices, to_next(): return lax.ppermute(x, SECTION, route)  3.51 us
    unnamed x14, local copies, waits for them, and re-layouts  3.5 us
    pallas_call x1, Pallas kernels, on_device(): call(dual_later, [local, partials, line], [SMEM, SMEM] + [VMEM] * 4)  2.57 us
    ppermute x2, waiting for transfers between devices, to_twin(): return lax.ppermute(x, TWIN, [(0, 1), (1, 0)])  2.27 us
  transfers between devices with their start and end apart: 6, of which 4 were waited for; matrix products, arithmetic and copies ran while one was open for 0% of the time, Pallas kernels for 4%

profile of v1, /device:TPU:1, one launch (start us, length us, event | category | flops | bytes accessed | tf_op | source)
XLA Modules:
  0.0 107.1 jit_solution(11478186351210077320)
XLA Ops:
  0.7 0.7 subtract_select_fusion
  1.4 0.1 copy.13
  1.5 0.1 reshape.19.index_ref
  1.6 0.0 copy-start
  1.6 2.8 %copy-done = f32[8,2,6,128,128]{4,3,2,1,0:T(8,128)S(1)} copy-done((f32[8,2,6,128,128]{4,3,2,1,0:T(8,128)S(1)}, f32[8,2,6,128,128]{4,3,2,1,0:T(8,128)}, u32[]{:S(2)}) %copy-start) | copy-done | bytes 6291480
  4.4 0.0 copy-start.1
  4.4 0.7 copy-done.1
  5.1 0.0 copy-start.3
  5.1 0.0 copy-start.4
  5.1 0.0 slice-start
  5.1 0.0 copy-start.2
  5.1 0.8 shard_map.95
  5.9 5.3 %collective-permute-start = (f32[64,128]{1,0:T(8,128)S(1)}, f32[64,128]{1,0:T(8,128)S(1)}, u32[]{:S(2)}, u32[]{:S(2)}) collective-permute-start(f32[64,128]{1,0:T(8,128)S(1)} %get-tuple-element.19), channel_id=1, source_target_pairs={{32,0},{64,32},{96,64},{128,96},{160,128},{192,160},{224,192},{33,... | collective-permute-start | bytes 98312 | tf_op jit(solution)/shard_map/ppermute | solution.py:277
  11.1 0.0 slice-start.1
  11.2 1.2 %shard_map.96.partial_in = f32[640,128]{1,0:T(8,128)S(1)} custom-call(s32[96]{0:T(128)S(1)} %reshape.19.index_ref, f32[8,2,6,128,128]{4,3,2,1,0:T(8,128)S(1)} %copy-done, f32[8,256]{1,0:T(8,128)S(1)} %copy-done.1, f32[64,128]{1,0:T(8,128)S(1)} %get-tuple-element.18.own_ref), custom_call_target="tpu_custom_call" | custom-call | tf_op jit(solution)/shard_map/pallas_call | solution.py:314
  12.3 0.2 collective-permute-done.carried_ref
  12.5 15.0 %all_to_all.25.pieces_ref = f32[16,40,128]{2,1,0:T(8,128)S(1)} all-to-all(f32[16,40,128]{2,1,0:T(8,128)S(1)} %bitcast.14), channel_id=1, replica_groups=mesh['section_0'=4,'section_1'=2,'dom_0'=4,'dom_1'=2,'dom_2'=4] {'dom_0'..., dimensions={0} | all-to-all | bytes 655360 | tf_op jit(solution)/shard_map/all_to_all | solution.py:285
  27.6 0.0 copy-done.3
  27.6 0.0 copy-done.4
  27.6 7.0 %collective-permute-start.1 = (f32[64,128]{1,0:T(8,128)S(1)}, f32[64,128]{1,0:T(8,128)S(1)}, u32[]{:S(2)}, u32[]{:S(2)}) collective-permute-start(f32[64,128]{1,0:T(8,128)S(1)} %shard_map.98.pack_ref), channel_id=1, source_target_pairs={{0,4},{4,0},{1,5},{5,1},{2,6},{6,2},{3,7},{7,3},{8,12},{12,8},{9,1... | collective-permute-start | bytes 98312 | tf_op jit(solution)/shard_map/ppermute | solution.py:281
  35.2 1.1 %collective-permute-done.1.other_ref = f32[64,128]{1,0:T(8,128)S(1)} collective-permute-done((f32[64,128]{1,0:T(8,128)S(1)}, f32[64,128]{1,0:T(8,128)S(1)}, u32[]{:S(2)}, u32[]{:S(2)}) %collective-permute-start.1) | collective-permute-done | bytes 32800 | tf_op jit(solution)/shard_map/ppermute | solution.py:281
  36.4 10.1 %all_to_all.26 = f32[16,32,128]{2,1,0:T(8,128)S(1)} all-to-all(f32[16,32,128]{2,1,0:T(8,128)S(1)} %get-tuple-element.20), channel_id=1, replica_groups=mesh['section_0'=4,'section_1'=2,'dom_0'=4,'dom_1'=2,'dom_2'=4] {'dom_0'..., dimensions={0} | all-to-all | bytes 524288 | tf_op jit(solution)/shard_map/all_to_all | solution.py:285
  46.6 6.1 %collective-permute-start.2 = (f32[64,128]{1,0:T(8,128)S(1)}, f32[64,128]{1,0:T(8,128)S(1)}, u32[]{:S(2)}, u32[]{:S(2)}) collective-permute-start(f32[64,128]{1,0:T(8,128)S(1)} %bitcast.22), channel_id=1, source_target_pairs={{0,32},{32,64},{64,96},{96,128},{128,160},{160,192},{192,224},{1,3... | collective-permute-start | bytes 98312 | tf_op jit(solution)/shard_map/ppermute | solution.py:277
  52.7 0.0 slice-done
  52.7 0.0 copy-done.2
  52.7 0.0 slice-done.1
  52.7 2.6 %shard_map.100 = (f32[8,256]{1,0:T(8,128)S(1)}, f32[640,128]{1,0:T(8,128)S(1)}, f32[1,128]{1,0:T(1,128)S(1)}) custom-call(s32[96]{0:T(128)S(1)} %reshape.19.index_ref, f32[1]{0:T(128)S(6)} %copy.20.weight_ref, f32[8,2,6,128,128]{4,3,2,1,0:T(8,128)S(1)} %bitcast.13, f32[512,128]{1,0:T(8,128)S(1)} %bitcast.16, f32[8,256]{1,0:T(8,128)S(1)} %copy-done.1, ...), custom_call_target="tpu_custom_call" | custom-call | tf_op jit(solution)/shard_map/pallas_call | solution.py:324
  55.3 0.0 collective-permute-done.2.carried_ref
  55.3 0.9 shard_map.101
  56.2 1.9 %collective-permute-start.3 = (f32[64,128]{1,0:T(8,128)S(1)}, f32[64,128]{1,0:T(8,128)S(1)}, u32[]{:S(2)}, u32[]{:S(2)}) collective-permute-start(f32[64,128]{1,0:T(8,128)S(1)} %get-tuple-element.24), channel_id=1, source_target_pairs={{32,0},{64,32},{96,64},{128,96},{160,128},{192,160},{224,192},{33,... | collective-permute-start | bytes 98312 | tf_op jit(solution)/shard_map/ppermute | solution.py:277
  58.1 3.3 %collective-permute-done.3.carried_ref = f32[64,128]{1,0:T(8,128)S(1)} collective-permute-done((f32[64,128]{1,0:T(8,128)S(1)}, f32[64,128]{1,0:T(8,128)S(1)}, u32[]{:S(2)}, u32[]{:S(2)}) %collective-permute-start.3) | collective-permute-done | bytes 32800 | tf_op jit(solution)/shard_map/ppermute | solution.py:277
  61.5 10.9 %all_to_all.27.pieces_ref = f32[16,40,128]{2,1,0:T(8,128)S(1)} all-to-all(f32[16,40,128]{2,1,0:T(8,128)S(1)} %bitcast.21), channel_id=1, replica_groups=mesh['section_0'=4,'section_1'=2,'dom_0'=4,'dom_1'=2,'dom_2'=4] {'dom_0'..., dimensions={0} | all-to-all | bytes 655360 | tf_op jit(solution)/shard_map/all_to_all | solution.py:285
  72.4 5.6 %collective-permute-start.4 = (f32[40,128]{1,0:T(8,128)S(1)}, f32[40,128]{1,0:T(8,128)S(1)}, u32[]{:S(2)}, u32[]{:S(2)}) collective-permute-start(f32[40,128]{1,0:T(8,128)S(1)} %shard_map.103.sum_ref), channel_id=1, source_target_pairs={{0,4},{4,0},{1,5},{5,1},{2,6},{6,2},{3,7},{7,3},{8,12},{12,8},{9,1... | collective-permute-start | bytes 61448 | tf_op jit(solution)/shard_map/ppermute | solution.py:281
  78.0 1.2 %collective-permute-done.4.other_ref = f32[40,128]{1,0:T(8,128)S(1)} collective-permute-done((f32[40,128]{1,0:T(8,128)S(1)}, f32[40,128]{1,0:T(8,128)S(1)}, u32[]{:S(2)}, u32[]{:S(2)}) %collective-permute-start.4) | collective-permute-done | bytes 20512 | tf_op jit(solution)/shard_map/ppermute | solution.py:281
  79.2 10.2 %all_to_all.28.moves_ref = f32[8,8,128]{2,1,0:T(8,128)S(1)} all-to-all(f32[8,8,128]{2,1,0:T(8,128)S(1)} %shard_map.104), channel_id=1, replica_groups=mesh['section_0'=4,'section_1'=2,'dom_0'=4,'dom_1'=2,'dom_2'=4] {'sectio..., dimensions={0} | all-to-all | bytes 65536 | tf_op jit(solution)/shard_map/all_to_all | solution.py:285
  89.4 0.7 shard_map.105
  90.1 10.2 %all_to_all.29 = f32[16,32,128]{2,1,0:T(8,128)S(1)} all-to-all(f32[16,32,128]{2,1,0:T(8,128)S(1)} %get-tuple-element.31), channel_id=1, replica_groups=mesh['section_0'=4,'section_1'=2,'dom_0'=4,'dom_1'=2,'dom_2'=4] {'dom_0'..., dimensions={0} | all-to-all | bytes 524288 | tf_op jit(solution)/shard_map/all_to_all | solution.py:285
  100.4 4.4 %collective-permute-start.5 = (f32[64,128]{1,0:T(8,128)S(1)}, f32[64,128]{1,0:T(8,128)S(1)}, u32[]{:S(2)}, u32[]{:S(2)}) collective-permute-start(f32[64,128]{1,0:T(8,128)S(1)} %bitcast.23), channel_id=1, source_target_pairs={{0,32},{32,64},{64,96},{96,128},{128,160},{160,192},{192,224},{1,3... | collective-permute-start | bytes 98312 | tf_op jit(solution)/shard_map/ppermute | solution.py:277
  104.7 1.0 shard_map.106.product_ref
  105.7 0.0 collective-permute-done.5.carried_ref
  105.7 1.3 %shard_map.107 = f32[8,256]{1,0:T(8,128)} custom-call(s32[96]{0:T(128)S(1)} %reshape.19.index_ref, f32[8,2,6,128,128]{4,3,2,1,0:T(8,128)S(1)} %bitcast.13, f32[512,128]{1,0:T(8,128)S(1)} %bitcast.20, f32[64,128]{1,0:T(8,128)S(1)} %collective-permute-done.5.carried_ref, f32[8,128]{1,0:T(8,128)S(1)} %get-tuple-element.32.steps_ref, ...), custom_call_target="tpu_custom_call" | custom-call | tf_op jit(solution)/shard_map/pallas_call | solution.py:345
  (11 shorter events, 0.2 us)
Async XLA Ops:
  1.6 2.8 %copy-start = (f32[8,2,6,128,128]{4,3,2,1,0:T(8,128)S(1)}, f32[8,2,6,128,128]{4,3,2,1,0:T(8,128)}, u32[]{:S(2)}) copy-start(f32[8,2,6,128,128]{4,3,2,1,0:T(8,128)} %blocks_ref.11) | copy-start | bytes 18874372
  4.4 0.7 copy-start.1
  5.1 22.5 %copy-start.3 = (f32[8,256]{1,0:T(8,128)S(1)}, f32[8,256]{1,0:T(8,128)}, u32[]{:S(2)}) copy-start(f32[8,256]{1,0:T(8,128)} %primal_ref.1) | copy-start | bytes 24580
  5.1 22.5 %copy-start.4 = (f32[8,256]{1,0:T(8,128)S(1)}, f32[8,256]{1,0:T(8,128)}, u32[]{:S(2)}) copy-start(f32[8,256]{1,0:T(8,128)} %cost_ref.1) | copy-start | bytes 24580
  5.1 47.6 %slice-start = ((s8[6291456]{0:T(1024)(128)(4,1)}), s8[4194304]{0:T(1024)(128)(4,1)S(1)}, s32[]{:S(2)}) async-start(s8[6291456]{0:T(1024)(128)(4,1)} %bitcast.12), calls=%async_computation.5 | async-start | bytes 8388608
  5.1 47.6 %copy-start.2 = (f32[8,256]{1,0:T(8,128)S(1)}, f32[8,256]{1,0:T(8,128)}, u32[]{:S(2)}) copy-start(f32[8,256]{1,0:T(8,128)} %demand_ref.5) | copy-start | bytes 24580
  5.9 6.7 %collective-permute-start = (f32[64,128]{1,0:T(8,128)S(1)}, f32[64,128]{1,0:T(8,128)S(1)}, u32[]{:S(2)}, u32[]{:S(2)}) collective-permute-start(f32[64,128]{1,0:T(8,128)S(1)} %get-tuple-element.19), channel_id=1, source_target_pairs={{32,0},{64,32},{96,64},{128,96},{160,128},{192,160},{224,192},{33,... | collective-permute-start | bytes 98312 | tf_op jit(solution)/shard_map/ppermute | solution.py:277
  11.1 41.5 %slice-start.1 = ((s8[6291456]{0:T(1024)(128)(4,1)}), s8[2097152]{0:T(1024)(128)(4,1)S(1)}, s32[]{:S(2)}) async-start(s8[6291456]{0:T(1024)(128)(4,1)} %bitcast.12), calls=%async_computation.6 | async-start | bytes 4194304
  27.6 8.7 %collective-permute-start.1 = (f32[64,128]{1,0:T(8,128)S(1)}, f32[64,128]{1,0:T(8,128)S(1)}, u32[]{:S(2)}, u32[]{:S(2)}) collective-permute-start(f32[64,128]{1,0:T(8,128)S(1)} %shard_map.98.pack_ref), channel_id=1, source_target_pairs={{0,4},{4,0},{1,5},{5,1},{2,6},{6,2},{3,7},{7,3},{8,12},{12,8},{9,1... | collective-permute-start | bytes 98312 | tf_op jit(solution)/shard_map/ppermute | solution.py:281
  46.6 8.7 %collective-permute-start.2 = (f32[64,128]{1,0:T(8,128)S(1)}, f32[64,128]{1,0:T(8,128)S(1)}, u32[]{:S(2)}, u32[]{:S(2)}) collective-permute-start(f32[64,128]{1,0:T(8,128)S(1)} %bitcast.22), channel_id=1, source_target_pairs={{0,32},{32,64},{64,96},{96,128},{128,160},{160,192},{192,224},{1,3... | collective-permute-start | bytes 98312 | tf_op jit(solution)/shard_map/ppermute | solution.py:277
  56.2 5.2 %collective-permute-start.3 = (f32[64,128]{1,0:T(8,128)S(1)}, f32[64,128]{1,0:T(8,128)S(1)}, u32[]{:S(2)}, u32[]{:S(2)}) collective-permute-start(f32[64,128]{1,0:T(8,128)S(1)} %get-tuple-element.24), channel_id=1, source_target_pairs={{32,0},{64,32},{96,64},{128,96},{160,128},{192,160},{224,192},{33,... | collective-permute-start | bytes 98312 | tf_op jit(solution)/shard_map/ppermute | solution.py:277
  72.4 6.8 %collective-permute-start.4 = (f32[40,128]{1,0:T(8,128)S(1)}, f32[40,128]{1,0:T(8,128)S(1)}, u32[]{:S(2)}, u32[]{:S(2)}) collective-permute-start(f32[40,128]{1,0:T(8,128)S(1)} %shard_map.103.sum_ref), channel_id=1, source_target_pairs={{0,4},{4,0},{1,5},{5,1},{2,6},{6,2},{3,7},{7,3},{8,12},{12,8},{9,1... | collective-permute-start | bytes 61448 | tf_op jit(solution)/shard_map/ppermute | solution.py:281
  100.4 5.4 %collective-permute-start.5 = (f32[64,128]{1,0:T(8,128)S(1)}, f32[64,128]{1,0:T(8,128)S(1)}, u32[]{:S(2)}, u32[]{:S(2)}) collective-permute-start(f32[64,128]{1,0:T(8,128)S(1)} %bitcast.23), channel_id=1, source_target_pairs={{0,32},{32,64},{64,96},{96,128},{128,160},{160,192},{192,224},{1,3... | collective-permute-start | bytes 98312 | tf_op jit(solution)/shard_map/ppermute | solution.py:277

commit v2 on v1

v2 whole, which is shorter than its diff:
```python
import functools

import jax
import jax.numpy as jnp
from jax import lax
from jax.experimental import pallas as pl
from jax.experimental.pallas import tpu as pltpu
from jax.sharding import Mesh
from jax.sharding import PartitionSpec as P

AXES = ("section_0", "section_1", "dom_0", "dom_1", "dom_2")
SECTION = ("section_0", "section_1")
DOM = ("dom_0", "dom_1", "dom_2")
PLANE = ("dom_0", "dom_2")
TWIN = "dom_1"
LINE = ("section_0", "section_1", "dom_1")

step_scale = 0.4
epsilon = 1e-06

PEERS = 16
PERIODS_HERE = 8
LATER = tuple(range(1, 8))
CHUNK = 32
PIECE = 40

f32 = jnp.float32
VMEM = pl.BlockSpec(memory_space=pltpu.VMEM)
HBM = pl.BlockSpec(memory_space=pltpu.HBM)
SMEM = pl.BlockSpec(memory_space=pltpu.SMEM)
PARAMS = pltpu.CompilerParams(vmem_limit_bytes=32 << 20)


def shaped(*shape):
    return jax.ShapeDtypeStruct(shape, f32)


def call(kernel, outs, ins, scratch=(), places=None):
    return pl.pallas_call(
        kernel,
        out_shape=outs,
        in_specs=ins,
        out_specs=places or jax.tree.map(lambda _: VMEM, outs),
        scratch_shapes=list(scratch),
        compiler_params=PARAMS,
    )


def columns_of(ref):
    rows = jnp.concatenate([ref[:, :128], ref[:, 128:], jnp.zeros((112, 128), f32)], axis=0)
    return rows.T


def store_rows(ref, rows):
    ref[:, :128] = rows[0:8]
    ref[:, 128:] = rows[8:16]


def transposed_product(block, wide):
    return jnp.sum(block * wide, axis=0, keepdims=True)


def row_of(index_ref, t, r, k, spread):
    row = index_ref[t * 12 + r * 6 + k]
    if not spread:
        return row
    if t > 0:
        return row + (row >> 5) * (PIECE - CHUNK)
    place = row & 63
    inside = place & 3
    return (place >> 2) * PIECE + jnp.where(row < 64, inside * 8, inside + CHUNK)


def add_terms(blocks_ref, index_ref, dest_ref, t, r, wide, spread=True):
    for k in range(6):
        row = row_of(index_ref, t, r, k, spread)
        dest_ref[pl.ds(row, 1), :] += transposed_product(blocks_ref[t, r, k], wide)


def row_product(blocks_ref, index_ref, source_ref, t, r, spread=False):
    total = jnp.zeros((128, 128), f32)
    for k in range(6):
        row = row_of(index_ref, t, r, k, spread)
        total += blocks_ref[t, r, k] * source_ref[pl.ds(row, 1), :]
    return jnp.sum(total, axis=1, keepdims=True)


def adjoint_first(
    column_in, period_in, blocks_ref, dual_ref, index_ref, own_ref, carry_ref,
    column_ref, period_ref, block_rows, dual_rows, terms, arrived,
):
    get_column = pltpu.make_async_copy(column_in, column_ref, arrived.at[2])
    get_period = pltpu.make_async_copy(period_in, period_ref, arrived.at[3])
    get_column.start()
    get_period.start()
    get_blocks = pltpu.make_async_copy(blocks_ref.at[0], block_rows.at[0], arrived.at[0])
    get_dual = pltpu.make_async_copy(dual_ref, dual_rows, arrived.at[1])
    get_dual.start()
    get_blocks.start()
    terms[...] = jnp.zeros_like(terms)
    first_period = lax.axis_index(SECTION) * PERIODS_HERE
    get_column.wait()
    get_period.wait()
    for t in range(PERIODS_HERE):
        for r in range(2):
            for k in range(6):
                c = column_ref[k, r, t]
                before = first_period + t - period_ref[k, r, t]
                place = ((c >> 4) * 4 + ((c >> 1) & 3)) * 4 + ((c >> 3) & 1) * 2 + (c & 1)
                row = place + 64 * before if t == 0 else place * 8 + t - before
                index_ref[t * 12 + r * 6 + k] = row
    get_dual.wait()
    columns = columns_of(dual_rows)
    get_blocks.wait()
    for r in range(2):
        wide = jnp.broadcast_to(columns[:, r * 8 : r * 8 + 1], (128, 128))
        add_terms(block_rows, index_ref, terms, 0, r, wide, False)
    own_ref[...] = terms[0:64]
    carry_ref[...] = terms[64:128]


def adjoint_later(index_ref, blocks_ref, dual_ref, own_ref, partial_ref):
    partial_ref[...] = jnp.zeros_like(partial_ref)
    for p in range(PEERS):
        partial_ref[pl.ds(p * PIECE, 4, stride=8), :] = own_ref[p * 4 : p * 4 + 4]
    columns = columns_of(dual_ref)
    for t in LATER:
        for r in range(2):
            place = r * 8 + t
            wide = jnp.broadcast_to(columns[:, place : place + 1], (128, 128))
            add_terms(blocks_ref, index_ref, partial_ref, t, r, wide)


def add_carried(partial_in, carried_ref, partial_ref):
    partial_ref[...] = partial_in[...]
    for p in range(PEERS):
        partial_ref[pl.ds(p * PIECE + 7, 4, stride=8), :] += carried_ref[p * 4 : p * 4 + 4]


def total_of(pieces_ref):
    total = pieces_ref[0]
    for p in range(1, PEERS):
        total = total + pieces_ref[p]
    return total


def sum_and_pack(pieces_ref, primal_ref, cost_ref, pack_ref):
    pack_ref[0:CHUNK, :] = total_of(pieces_ref)[0:CHUNK]
    pack_ref[32:40, :] = primal_ref[:, :128]
    pack_ref[40:48, :] = primal_ref[:, 128:]
    pack_ref[48:56, :] = cost_ref[:, :128]
    pack_ref[56:64, :] = cost_ref[:, 128:]


def sum_and_tiles(pieces_ref, primal_one_ref, cost_ref, sum_ref, tiles_ref, tile):
    total = total_of(pieces_ref)
    sum_ref[...] = total
    last = pl.ds(7, 4, stride=8)
    tile[0:4, :] = total[32:36]
    tile[4:8, :] = sum_ref[last, :] - 0.5 * cost_ref[last, :]
    tile[8:12, :] = primal_one_ref[last, :]
    tile[12:16, :] = total[36:40]
    to_all(tiles_ref, tile[...])


def both_twins(own, other):
    first = lax.axis_index(TWIN) == 0
    return jnp.concatenate(
        [jnp.where(first, own, other), jnp.where(first, other, own)], axis=0
    )


def to_all(ref, value):
    for p in range(PEERS):
        ref[p] = value


def primal_step(weight_ref, pack_ref, other_ref, copies_ref, primal_one_ref, cost_ref, move_ref):
    tau = step_scale / jnp.full((CHUNK, 128), weight_ref[0], f32)
    product = pack_ref[0:32] + other_ref[0:32]
    start = both_twins(pack_ref[32:48], other_ref[32:48])
    cost = both_twins(pack_ref[48:64], other_ref[48:64])
    primal_one = jnp.maximum(0.0, start - tau * (cost - product))
    primal_one_ref[...] = primal_one
    cost_ref[...] = cost
    move_ref[...] = 0.5 * jnp.sum((primal_one - start) ** 2, axis=0, keepdims=True)
    to_all(copies_ref, 2.0 * primal_one - start)


def dual_later(
    index_ref, weight_ref, blocks_ref, field_ref, dual_ref, demand_ref, dual_one_ref, partial_ref, move_ref
):
    partial_ref[...] = jnp.zeros_like(partial_ref)
    sigma = step_scale * weight_ref[0]
    start = columns_of(dual_ref)
    demand = columns_of(demand_ref)
    lane = lax.broadcasted_iota(jnp.int32, (128, 128), 1)
    result = start
    for t in LATER:
        for r in range(2):
            place = r * 8 + t
            here = slice(place, place + 1)
            product = row_product(blocks_ref, index_ref, field_ref, t, r)
            dual_one = start[:, here] + sigma * (demand[:, here] - product)
            wide = jnp.broadcast_to(dual_one, (128, 128))
            result = jnp.where(lane == place, wide, result)
            add_terms(blocks_ref, index_ref, partial_ref, t, r, wide)
    move_ref[...] = jnp.sum((result - start).T ** 2, axis=0, keepdims=True)
    store_rows(dual_one_ref, result.T)


def first_rows(field_ref, carried_ref, rows):
    rows[0:64, :] = field_ref[pl.ds(0, 64, stride=8), :]
    rows[64:128, :] = carried_ref[...]


def dual_first(
    index_ref, weight_ref, blocks_ref, field_ref, carried_ref, dual_ref, demand_ref, later_ref, partial_in,
    move_x, move_a, dual_one_ref, partial_ref, rows,
):
    first_rows(field_ref, carried_ref, rows)
    partial_ref[...] = partial_in[...]
    sigma = step_scale * weight_ref[0]
    start = columns_of(dual_ref)
    demand = columns_of(demand_ref)
    later = columns_of(later_ref)
    lane = lax.broadcasted_iota(jnp.int32, (128, 128), 1)
    result = start
    for r in range(2):
        here = slice(r * 8, r * 8 + 1)
        product = row_product(blocks_ref, index_ref, rows, 0, r)
        dual_one = start[:, here] + sigma * (demand[:, here] - product)
        wide = jnp.broadcast_to(dual_one, (128, 128))
        result = jnp.where(lane == r * 8, wide, result)
        later = jnp.where(lane == r * 8, wide, later)
        add_terms(blocks_ref, index_ref, partial_ref, 0, r, wide)
    store_rows(dual_one_ref, later.T)
    move = jnp.sum((result - start).T ** 2, axis=0, keepdims=True) + move_a[...]
    moves = jnp.concatenate([move_x[...], move], 0)
    for p in range(PEERS):
        partial_ref[p * PIECE + 36 : p * PIECE + 38, :] = moves


def primal_last(
    weight_ref, tiles_ref, sum_ref, other_ref, primal_one_ref, cost_ref, copies_ref, primal_ref, steps_ref,
    gradient,
):
    section = lax.axis_index(SECTION)
    tile = tiles_ref[0, 8:16]
    for d in range(1, PEERS):
        tile = tile + tiles_ref[d, 8:16]
    move = jnp.broadcast_to(jnp.sum(tile, axis=1, keepdims=True), (8, 128))
    move_primal, move_dual = move[4:5], move[5:6]
    weight = jnp.full((1, 128), weight_ref[0], f32)
    omega = jnp.sqrt(weight * jnp.sqrt((move_dual + epsilon) / (move_primal + epsilon)))
    tau = step_scale / omega
    steps_ref[...] = jnp.broadcast_to(step_scale * omega, (8, 128))

    above = 2 * jnp.minimum(section + 1, 7)
    carried = tiles_ref[above, 0:4] + tiles_ref[above + 1, 0:4]
    gradient[...] = cost_ref[...] - (sum_ref[0:CHUNK] + other_ref[0:CHUNK])
    gradient[pl.ds(7, 4, stride=8), :] -= jnp.where(section < 7, carried, 0.0)
    primal_one = primal_one_ref[...]
    primal = jnp.maximum(0.0, primal_one - tau * gradient[...])
    primal_ref[...] = primal
    field = 2.0 * primal - primal_one

    below = 2 * jnp.maximum(section - 1, 0)
    product = tiles_ref[below, 4:8] + tiles_ref[below + 1, 4:8] + sum_ref[32:36] + other_ref[32:36]
    before_one = tiles_ref[below, 8:12]
    before = jnp.maximum(0.0, before_one + tau * product)
    before_field = 2.0 * before - before_one
    to_all(copies_ref, jnp.concatenate([field, before_field, jnp.zeros((4, 128), f32)], 0))


def last_dual(
    index_ref, blocks_ref, field_ref, steps_ref, dual_ref, demand_ref, primal_ref, primal_out, dual_out
):
    first = lax.axis_index(TWIN) == 0
    primal_out[:, :128] = jnp.where(first, primal_ref[0:8], primal_ref[16:24])
    primal_out[:, 128:] = jnp.where(first, primal_ref[8:16], primal_ref[24:32])
    lane = lax.broadcasted_iota(jnp.int32, (128, 128), 1)
    result = jnp.zeros((128, 128), f32)
    for t in range(PERIODS_HERE):
        for r in range(2):
            product = row_product(blocks_ref, index_ref, field_ref, t, r, True)
            result = jnp.where(lane == r * 8 + t, jnp.broadcast_to(product, (128, 128)), result)
    result = result.T
    sigma = steps_ref[...]
    for r in range(2):
        part = slice(r * 128, r * 128 + 128)
        dual_out[:, part] = dual_ref[:, part] + sigma * (
            demand_ref[:, part] - result[r * 8 : r * 8 + 8]
        )


def to_next(x, distance):
    route = [(i - distance, i) for i in range(8) if 0 <= i - distance < 8]
    return lax.ppermute(x, SECTION, route)


def to_twin(x):
    return lax.ppermute(x, TWIN, [(0, 1), (1, 0)])


def exchange(pieces, axis):
    return lax.all_to_all(pieces, axis, split_axis=0, concat_axis=0, tiled=True)


def in_hbm(x):
    return pltpu.with_memory_space_constraint(x, pltpu.HBM)


def on_device(
    blocks, column_index, block_period, cost_vector, demand, primal_start, dual_start, primal_weight
):
    terms = pltpu.VMEM((128, 128), f32)
    half = shaped(64, 128)
    line = shaped(1, 128)
    partials = shaped(PEERS * PIECE, 128)
    chunk = shaped(CHUNK, 128)
    copies = shaped(PEERS, CHUNK, 128)
    local = shaped(8, 256)

    index, own, carry = call(
        adjoint_first,
        [jax.ShapeDtypeStruct((96,), jnp.int32), half, half],
        [HBM] * 4,
        [
            pltpu.SMEM((6, 2, 8), jnp.int32),
            pltpu.SMEM((6, 2, 8), jnp.int32),
            pltpu.VMEM((1, 2, 6, 128, 128), f32),
            pltpu.VMEM((8, 256), f32),
            terms,
            pltpu.SemaphoreType.DMA((4,)),
        ],
        [SMEM, VMEM, VMEM],
    )(
        in_hbm(column_index.transpose(2, 1, 0)),
        in_hbm(block_period.transpose(2, 1, 0)),
        in_hbm(blocks),
        in_hbm(dual_start),
    )
    carried = to_next(carry, -1)
    partial = call(adjoint_later, partials, [SMEM, VMEM, VMEM, VMEM])(index, blocks, dual_start, own)
    partial = call(add_carried, partials, [VMEM, VMEM])(partial, carried)
    pieces = exchange(partial.reshape(PEERS, PIECE, 128), PLANE)
    pack = call(sum_and_pack, shaped(64, 128), [VMEM] * 3)(pieces, primal_start, cost_vector)
    other = to_twin(pack)
    send, primal_one, cost, move_primal = call(
        primal_step, [copies, chunk, chunk, line], [SMEM, VMEM, VMEM]
    )(primal_weight, pack, other)
    field = exchange(send, PLANE).reshape(PEERS * CHUNK, 128)
    carried = to_next(field.reshape(64, 8, 128)[:, 7], 1)
    dual_some, partial, move_a = call(
        dual_later, [local, partials, line], [SMEM, SMEM] + [VMEM] * 4
    )(index, primal_weight, blocks, field, dual_start, demand)
    dual_one, partial = call(
        dual_first, [local, partials], [SMEM, SMEM] + [VMEM] * 9, [terms]
    )(
        index, primal_weight, blocks, field, carried, dual_start, demand, dual_some, partial,
        move_primal, move_a,
    )
    pieces = exchange(partial.reshape(PEERS, PIECE, 128), PLANE)
    tile = pltpu.VMEM((16, 128), f32)
    total, tiles = call(
        sum_and_tiles, [shaped(PIECE, 128), shaped(PEERS, 16, 128)], [VMEM] * 3, [tile]
    )(pieces, primal_one, cost)
    other = to_twin(total)
    tiles = exchange(tiles, LINE)
    send, primal, steps = call(
        primal_last,
        [shaped(PEERS, PIECE, 128), chunk, shaped(8, 128)],
        [SMEM] + [VMEM] * 5,
        [pltpu.VMEM((CHUNK, 128), f32)],
    )(primal_weight, tiles, total, other, primal_one, cost)
    field = exchange(send, PLANE).reshape(PEERS * PIECE, 128)
    primal_final, dual_final = call(last_dual, [local, local], [SMEM] + [VMEM] * 6)(
        index, blocks, field, steps, dual_one, demand, primal
    )
    return primal_final, dual_final


def solution(mesh):
    finer = Mesh(mesh.devices.reshape(4, 2, 4, 2, 4), AXES)
    return jax.shard_map(
        on_device,
        mesh=finer,
        in_specs=(
            P(SECTION, DOM, None, None, None),
            P(SECTION, DOM, None),
            P(SECTION, DOM, None),
            P(SECTION, DOM),
            P(SECTION, DOM),
            P(SECTION, DOM),
            P(SECTION, DOM),
            P(),
        ),
        out_specs=(P(SECTION, DOM), P(SECTION, DOM)),
        check_vma=False,
    )
```

time: 108 us -> 99.3 us (0.919)
  blocking collectives: 56.5 us -> 46.6 us
  starting transfers between devices: 30.3 us -> 32.8 us
    all_to_all x5 -> x4, blocking collectives: 56.5 us -> 46.6 us  [exchange(): return lax.all_to_all(pieces, axis, split_axis=0, concat_axis=0, tiled=True)]
    all_to_all x0 -> x1, starting transfers between devices: none -> 9.31 us  [exchange(): return lax.all_to_all(pieces, axis, split_axis=0, concat_axis=0, tiled=True)]
    ppermute x4 -> x2, starting transfers between devices: 17.7 us -> 11.2 us  [to_next(): return lax.ppermute(x, SECTION, route)]
    ppermute x4 -> x2, waiting for transfers between devices: 3.51 us -> 0.18 us  [to_next(): return lax.ppermute(x, SECTION, route)]
    ppermute x2, waiting for transfers between devices: 2.27 us -> 5.52 us  [to_twin(): return lax.ppermute(x, TWIN, [(0, 1), (1, 0)])]
    pallas_call x9 -> x6, Pallas kernels: 4.82 us -> 5.7 us  [the longest x1 2.21 us: on_device(): call(adjoint_first, [jax.ShapeDtypeStruct((96,), jnp.int32), half, half],...]
    unnamed x14 -> x12, local copies, waits for them, and re-layouts: 3.5 us -> 2.81 us
  transfers between devices with their start and end apart: 6 -> 5, of which waited for: 4 -> 3; matrix products, arithmetic and copies ran while one was open for 0% -> 0% of each run, Pallas kernels for 4% -> 4%
where the time goes in v2:
time: 99.3 us; the launch traced here: 98.9 us
  blocking collectives  46.6 us (47%)
  starting transfers between devices  32.8 us (33%)
  Pallas kernels  9.52 us (10%)
  waiting for transfers between devices  5.71 us (6%)
  local copies, waits for them, and re-layouts  2.84 us (3%)
  between operations  1.42 us (1%)
    all_to_all x4, blocking collectives, exchange(): return lax.all_to_all(pieces, axis, split_axis=0, concat_axis=0, tiled=True)  46.6 us
    ppermute x2, starting transfers between devices, to_twin(): return lax.ppermute(x, TWIN, [(0, 1), (1, 0)])  12.3 us
    ppermute x2, starting transfers between devices, to_next(): return lax.ppermute(x, SECTION, route)  11.2 us
    all_to_all x1, starting transfers between devices, exchange(): return lax.all_to_all(pieces, axis, split_axis=0, concat_axis=0, tiled=True)  9.31 us
    ppermute x2, waiting for transfers between devices, to_twin(): return lax.ppermute(x, TWIN, [(0, 1), (1, 0)])  5.52 us
    unnamed x12, local copies, waits for them, and re-layouts  2.81 us
    pallas_call x1, Pallas kernels, on_device(): call(dual_later, [local, partials, line], [SMEM, SMEM] + [VMEM] * 4)  2.6 us
    pallas_call x1, Pallas kernels, on_device(): call(adjoint_first, [jax.ShapeDtypeStruct((96,), jnp.int32), half, half],...  2.21 us
  transfers between devices with their start and end apart: 5, of which 3 were waited for; matrix products, arithmetic and copies ran while one was open for 0% of the time, Pallas kernels for 4%

profile of v2, /device:TPU:1, one launch (start us, length us, event | category | flops | bytes accessed | tf_op | source)
XLA Modules:
  0.0 98.9 jit_solution(9724016075607902602)
XLA Ops:
  0.6 0.0 copy-start
  0.6 0.0 copy-start.2
  0.7 0.0 copy-start.4
  0.7 0.0 copy-start.5
  0.7 0.0 copy-start.3
  0.7 2.2 %shard_map.95 = (s32[96]{0:T(128)S(1)}, f32[64,128]{1,0:T(8,128)S(1)}, f32[64,128]{1,0:T(8,128)S(1)}) custom-call(s32[6,2,8]{2,1,0:T(2,128)} %bitcast.17, s32[6,2,8]{2,1,0:T(2,128)} %bitcast.18, f32[8,2,6,128,128]{4,3,2,1,0:T(8,128)} %blocks_ref.9, f32[8,256]{1,0:T(8,128)} %dual_ref.7), custom_call_target="tpu_custom_call" | custom-call | tf_op jit(solution)/shard_map/pallas_call | solution.py:325
  2.9 5.1 %collective-permute-start = (f32[64,128]{1,0:T(8,128)S(1)}, f32[64,128]{1,0:T(8,128)S(1)}, u32[]{:S(2)}, u32[]{:S(2)}) collective-permute-start(f32[64,128]{1,0:T(8,128)S(1)} %get-tuple-element.21), channel_id=1, source_target_pairs={{32,0},{64,32},{96,64},{128,96},{160,128},{192,160},{224,192},{33,... | collective-permute-start | bytes 98312 | tf_op jit(solution)/shard_map/ppermute | solution.py:299
  8.1 0.0 copy-done
  8.1 0.0 copy-done.2
  8.1 1.2 %shard_map.96.partial_in = f32[640,128]{1,0:T(8,128)S(1)} custom-call(s32[96]{0:T(128)S(1)} %get-tuple-element.19.index_ref, f32[8,2,6,128,128]{4,3,2,1,0:T(8,128)S(1)} %copy-done, f32[8,256]{1,0:T(8,128)S(1)} %copy-done.2, f32[64,128]{1,0:T(8,128)S(1)} %get-tuple-element.20.own_ref), custom_call_target="tpu_custom_call" | custom-call | tf_op jit(solution)/shard_map/pallas_call | solution.py:345
  9.2 0.2 collective-permute-done.carried_ref
  9.5 15.0 %all_to_all.25.pieces_ref = f32[16,40,128]{2,1,0:T(8,128)S(1)} all-to-all(f32[16,40,128]{2,1,0:T(8,128)S(1)} %bitcast.14), channel_id=1, replica_groups=mesh['section_0'=4,'section_1'=2,'dom_0'=4,'dom_1'=2,'dom_2'=4] {'dom_0'..., dimensions={0} | all-to-all | bytes 655360 | tf_op jit(solution)/shard_map/all_to_all | solution.py:307
  24.5 0.0 copy-done.4
  24.5 0.0 copy-done.5
  24.5 7.0 %collective-permute-start.1 = (f32[64,128]{1,0:T(8,128)S(1)}, f32[64,128]{1,0:T(8,128)S(1)}, u32[]{:S(2)}, u32[]{:S(2)}) collective-permute-start(f32[64,128]{1,0:T(8,128)S(1)} %shard_map.98.pack_ref), channel_id=1, source_target_pairs={{0,4},{4,0},{1,5},{5,1},{2,6},{6,2},{3,7},{7,3},{8,12},{12,8},{9,1... | collective-permute-start | bytes 98312 | tf_op jit(solution)/shard_map/ppermute | solution.py:303
  32.2 1.1 %collective-permute-done.1.other_ref = f32[64,128]{1,0:T(8,128)S(1)} collective-permute-done((f32[64,128]{1,0:T(8,128)S(1)}, f32[64,128]{1,0:T(8,128)S(1)}, u32[]{:S(2)}, u32[]{:S(2)}) %collective-permute-start.1) | collective-permute-done | bytes 32800 | tf_op jit(solution)/shard_map/ppermute | solution.py:303
  33.3 10.1 %all_to_all.26 = f32[16,32,128]{2,1,0:T(8,128)S(1)} all-to-all(f32[16,32,128]{2,1,0:T(8,128)S(1)} %get-tuple-element.22), channel_id=1, replica_groups=mesh['section_0'=4,'section_1'=2,'dom_0'=4,'dom_1'=2,'dom_2'=4] {'dom_0'..., dimensions={0} | all-to-all | bytes 524288 | tf_op jit(solution)/shard_map/all_to_all | solution.py:307
  43.5 6.1 %collective-permute-start.2 = (f32[64,128]{1,0:T(8,128)S(1)}, f32[64,128]{1,0:T(8,128)S(1)}, u32[]{:S(2)}, u32[]{:S(2)}) collective-permute-start(f32[64,128]{1,0:T(8,128)S(1)} %bitcast.16), channel_id=1, source_target_pairs={{0,32},{32,64},{64,96},{96,128},{128,160},{160,192},{192,224},{1,3... | collective-permute-start | bytes 98312 | tf_op jit(solution)/shard_map/ppermute | solution.py:299
  49.6 0.0 copy-done.3
  49.6 2.6 %shard_map.100 = (f32[8,256]{1,0:T(8,128)S(1)}, f32[640,128]{1,0:T(8,128)S(1)}, f32[1,128]{1,0:T(1,128)S(1)}) custom-call(s32[96]{0:T(128)S(1)} %get-tuple-element.19.index_ref, f32[1]{0:T(128)S(6)} %copy.12.weight_ref, f32[8,2,6,128,128]{4,3,2,1,0:T(8,128)S(1)} %copy-done, f32[512,128]{1,0:T(8,128)S(1)} %bitcast.11, f32[8,256]{1,0:T(8,128)S(1)} %copy-done.2, ...), custom_call_target="tpu_custom_call" | custom-call | tf_op jit(solution)/shard_map/pallas_call | solution.py:355
  52.2 0.0 collective-permute-done.2.carried_ref
  52.2 0.9 shard_map.101
  53.1 10.5 %all_to_all.27.pieces_ref = f32[16,40,128]{2,1,0:T(8,128)S(1)} all-to-all(f32[16,40,128]{2,1,0:T(8,128)S(1)} %bitcast.15), channel_id=1, replica_groups=mesh['section_0'=4,'section_1'=2,'dom_0'=4,'dom_1'=2,'dom_2'=4] {'dom_0'..., dimensions={0} | all-to-all | bytes 655360 | tf_op jit(solution)/shard_map/all_to_all | solution.py:307
  63.6 0.7 shard_map.102
  64.3 9.3 %all-to-all-start.3 = ((f32[16,16,128]{2,1,0:T(8,128)}), f32[16,16,128]{2,1,0:T(8,128)S(1)}, u32[]{:S(2)}, u32[]{:S(2)}) async-start(f32[16,16,128]{2,1,0:T(8,128)} %get-tuple-element.30), calls=%async_computation.3 | async-start | bytes 262144 | tf_op jit(solution)/shard_map/all_to_all | solution.py:307
  73.6 5.3 %collective-permute-start.3 = (f32[40,128]{1,0:T(8,128)S(1)}, f32[40,128]{1,0:T(8,128)S(1)}, u32[]{:S(2)}, u32[]{:S(2)}) collective-permute-start(f32[40,128]{1,0:T(8,128)S(1)} %get-tuple-element.31.sum_ref), channel_id=1, source_target_pairs={{0,4},{4,0},{1,5},{5,1},{2,6},{6,2},{3,7},{7,3},{8,12},{12,8},{9,1... | collective-permute-start | bytes 61448 | tf_op jit(solution)/shard_map/ppermute | solution.py:303
  78.9 4.4 %collective-permute-done.3.other_ref = f32[40,128]{1,0:T(8,128)S(1)} collective-permute-done((f32[40,128]{1,0:T(8,128)S(1)}, f32[40,128]{1,0:T(8,128)S(1)}, u32[]{:S(2)}, u32[]{:S(2)}) %collective-permute-start.3) | collective-permute-done | bytes 20512 | tf_op jit(solution)/shard_map/ppermute | solution.py:303
  83.4 0.0 all-to-all-done.3.tiles_ref
  83.4 0.2 shard_map.103
  83.5 10.9 %all_to_all.28 = f32[16,40,128]{2,1,0:T(8,128)S(1)} all-to-all(f32[16,40,128]{2,1,0:T(8,128)S(1)} %get-tuple-element.32), channel_id=1, replica_groups=mesh['section_0'=4,'section_1'=2,'dom_0'=4,'dom_1'=2,'dom_2'=4] {'dom_0'..., dimensions={0} | all-to-all | bytes 655360 | tf_op jit(solution)/shard_map/all_to_all | solution.py:307
  94.4 0.0 copy-start.1
  94.4 2.8 %copy-done.1 = f32[8,2,6,128,128]{4,3,2,1,0:T(8,128)S(1)} copy-done((f32[8,2,6,128,128]{4,3,2,1,0:T(8,128)S(1)}, f32[8,2,6,128,128]{4,3,2,1,0:T(8,128)}, u32[]{:S(2)}) %copy-start.1) | copy-done | bytes 6291480
  97.2 1.7 %shard_map.104 = (f32[8,256]{1,0:T(8,128)}, f32[8,256]{1,0:T(8,128)}) custom-call(s32[96]{0:T(128)S(1)} %get-tuple-element.19.index_ref, f32[8,2,6,128,128]{4,3,2,1,0:T(8,128)S(1)} %copy-done.1, f32[640,128]{1,0:T(8,128)S(1)} %bitcast.13, f32[8,128]{1,0:T(8,128)S(1)} %get-tuple-element.33.steps_ref, f32[8,256]{1,0:T(8,128)S(1)} %get-tuple-element.34.dual_ref, ...), custom_call_target="tpu_custom_call" | custom-call | tf_op jit(solution)/shard_map/pallas_call | solution.py:378
  (4 shorter events, 0.1 us)
Async XLA Ops:
  0.6 7.4 %copy-start = (f32[8,2,6,128,128]{4,3,2,1,0:T(8,128)S(1)}, f32[8,2,6,128,128]{4,3,2,1,0:T(8,128)}, u32[]{:S(2)}) copy-start(f32[8,2,6,128,128]{4,3,2,1,0:T(8,128)} %blocks_ref.9) | copy-start | bytes 18874372
  0.6 7.4 %copy-start.2 = (f32[8,256]{1,0:T(8,128)S(1)}, f32[8,256]{1,0:T(8,128)}, u32[]{:S(2)}) copy-start(f32[8,256]{1,0:T(8,128)} %dual_ref.7) | copy-start | bytes 24580
  0.7 23.8 %copy-start.4 = (f32[8,256]{1,0:T(8,128)S(1)}, f32[8,256]{1,0:T(8,128)}, u32[]{:S(2)}) copy-start(f32[8,256]{1,0:T(8,128)} %primal_ref.1) | copy-start | bytes 24580
  0.7 23.8 %copy-start.5 = (f32[8,256]{1,0:T(8,128)S(1)}, f32[8,256]{1,0:T(8,128)}, u32[]{:S(2)}) copy-start(f32[8,256]{1,0:T(8,128)} %cost_ref.1) | copy-start | bytes 24580
  0.7 48.9 %copy-start.3 = (f32[8,256]{1,0:T(8,128)S(1)}, f32[8,256]{1,0:T(8,128)}, u32[]{:S(2)}) copy-start(f32[8,256]{1,0:T(8,128)} %demand_ref.5) | copy-start | bytes 24580
  2.9 6.5 %collective-permute-start = (f32[64,128]{1,0:T(8,128)S(1)}, f32[64,128]{1,0:T(8,128)S(1)}, u32[]{:S(2)}, u32[]{:S(2)}) collective-permute-start(f32[64,128]{1,0:T(8,128)S(1)} %get-tuple-element.21), channel_id=1, source_target_pairs={{32,0},{64,32},{96,64},{128,96},{160,128},{192,160},{224,192},{33,... | collective-permute-start | bytes 98312 | tf_op jit(solution)/shard_map/ppermute | solution.py:299
  24.5 8.7 %collective-permute-start.1 = (f32[64,128]{1,0:T(8,128)S(1)}, f32[64,128]{1,0:T(8,128)S(1)}, u32[]{:S(2)}, u32[]{:S(2)}) collective-permute-start(f32[64,128]{1,0:T(8,128)S(1)} %shard_map.98.pack_ref), channel_id=1, source_target_pairs={{0,4},{4,0},{1,5},{5,1},{2,6},{6,2},{3,7},{7,3},{8,12},{12,8},{9,1... | collective-permute-start | bytes 98312 | tf_op jit(solution)/shard_map/ppermute | solution.py:303
  43.5 8.7 %collective-permute-start.2 = (f32[64,128]{1,0:T(8,128)S(1)}, f32[64,128]{1,0:T(8,128)S(1)}, u32[]{:S(2)}, u32[]{:S(2)}) collective-permute-start(f32[64,128]{1,0:T(8,128)S(1)} %bitcast.16), channel_id=1, source_target_pairs={{0,32},{32,64},{64,96},{96,128},{128,160},{160,192},{192,224},{1,3... | collective-permute-start | bytes 98312 | tf_op jit(solution)/shard_map/ppermute | solution.py:299
  64.3 19.0 %all-to-all-start.3 = ((f32[16,16,128]{2,1,0:T(8,128)}), f32[16,16,128]{2,1,0:T(8,128)S(1)}, u32[]{:S(2)}, u32[]{:S(2)}) async-start(f32[16,16,128]{2,1,0:T(8,128)} %get-tuple-element.30), calls=%async_computation.3 | async-start | bytes 262144 | tf_op jit(solution)/shard_map/all_to_all | solution.py:307
  73.6 9.7 %collective-permute-start.3 = (f32[40,128]{1,0:T(8,128)S(1)}, f32[40,128]{1,0:T(8,128)S(1)}, u32[]{:S(2)}, u32[]{:S(2)}) collective-permute-start(f32[40,128]{1,0:T(8,128)S(1)} %get-tuple-element.31.sum_ref), channel_id=1, source_target_pairs={{0,4},{4,0},{1,5},{5,1},{2,6},{6,2},{3,7},{7,3},{8,12},{12,8},{9,1... | collective-permute-start | bytes 61448 | tf_op jit(solution)/shard_map/ppermute | solution.py:303
  94.4 2.8 %copy-start.1 = (f32[8,2,6,128,128]{4,3,2,1,0:T(8,128)S(1)}, f32[8,2,6,128,128]{4,3,2,1,0:T(8,128)}, u32[]{:S(2)}) copy-start(f32[8,2,6,128,128]{4,3,2,1,0:T(8,128)} %blocks_ref.9) | copy-start | bytes 18874372

commit v3 on v0

v3 whole, which is shorter than its diff:
```python
import functools

import jax
import jax.numpy as jnp
from jax import lax
from jax.experimental import pallas as pl
from jax.experimental.pallas import tpu as pltpu
from jax.sharding import Mesh
from jax.sharding import PartitionSpec as P

AXES = ("section_0", "section_1", "dom_0", "dom_1", "dom_2")
SECTION = ("section_0", "section_1")
DOM = ("dom_0", "dom_1", "dom_2")
PLANE = ("dom_0", "dom_2")
TWIN = "dom_1"
LINE = ("section_0", "dom_1")
CORE = "section_1"

step_scale = 0.4
epsilon = 1e-06

PEERS = 16
LINE_PEERS = 8
PERIODS_HERE = 8
CHUNK = 32
PIECE = 40
HALO = slice(32, 36)

f32 = jnp.float32
VMEM = pl.BlockSpec(memory_space=pltpu.VMEM)
HBM = pl.BlockSpec(memory_space=pltpu.HBM)
SMEM = pl.BlockSpec(memory_space=pltpu.SMEM)
PARAMS = pltpu.CompilerParams(vmem_limit_bytes=32 << 20)


def shaped(*shape):
    return jax.ShapeDtypeStruct(shape, f32)


def call(kernel, outs, ins, scratch=(), places=None):
    return pl.pallas_call(
        kernel,
        out_shape=outs,
        in_specs=ins,
        out_specs=places or jax.tree.map(lambda _: VMEM, outs),
        scratch_shapes=list(scratch),
        compiler_params=PARAMS,
    )


def columns_of(ref):
    rows = jnp.concatenate([ref[:, :128], ref[:, 128:], jnp.zeros((112, 128), f32)], axis=0)
    return rows.T


def store_rows(ref, rows):
    ref[:, :128] = rows[0:8]
    ref[:, 128:] = rows[8:16]


def row_of(index_ref, t, r, k):
    return pl.ds(index_ref[t * 12 + r * 6 + k], 1)


def add_terms(blocks_ref, index_ref, dest_ref, t, r, wide):
    for k in range(6):
        term = jnp.sum(blocks_ref[t, r, k] * wide, axis=0, keepdims=True)
        dest_ref[row_of(index_ref, t, r, k), :] += term


def all_products(blocks_ref, index_ref, source_ref):
    lane = lax.broadcasted_iota(jnp.int32, (128, 128), 1)
    result = jnp.zeros((128, 128), f32)
    for t in range(PERIODS_HERE):
        for r in range(2):
            total = jnp.zeros((128, 128), f32)
            for k in range(6):
                total += blocks_ref[t, r, k] * source_ref[row_of(index_ref, t, r, k), :]
            product = jnp.sum(total, axis=1, keepdims=True)
            result = jnp.where(lane == r * 8 + t, jnp.broadcast_to(product, (128, 128)), result)
    return result


def wide_column(columns, t, r):
    place = r * 8 + t
    return jnp.broadcast_to(columns[:, place : place + 1], (128, 128))


def adjoint_start(
    column_in, period_in, blocks_in, dual_in, index_ref, partial_ref, blocks_ref,
    column_ref, period_ref, dual_ref, arrived,
):
    get_column = pltpu.make_async_copy(column_in, column_ref, arrived.at[0])
    get_period = pltpu.make_async_copy(period_in, period_ref, arrived.at[1])
    get_dual = pltpu.make_async_copy(dual_in, dual_ref, arrived.at[2])
    get_blocks = [
        pltpu.make_async_copy(blocks_in.at[t], blocks_ref.at[t], arrived.at[3 + t])
        for t in range(PERIODS_HERE)
    ]
    for copy in [get_column, get_period, get_dual] + get_blocks:
        copy.start()
    partial_ref[...] = jnp.zeros_like(partial_ref)
    first_period = lax.axis_index(SECTION) * PERIODS_HERE
    get_column.wait()
    get_period.wait()
    for t in range(PERIODS_HERE):
        for r in range(2):
            for k in range(6):
                c = column_ref[k, r, t]
                before = first_period + t - period_ref[k, r, t]
                peer = (c >> 4) * 4 + ((c >> 1) & 3)
                inside = ((c >> 3) & 1) * 2 + (c & 1)
                row = inside * 8 + t - before
                if t == 0:
                    row = jnp.where(before == 0, inside * 8, inside + CHUNK)
                index_ref[t * 12 + r * 6 + k] = peer * PIECE + row
    get_dual.wait()
    columns = columns_of(dual_ref)
    for t in range(PERIODS_HERE):
        get_blocks[t].wait()
        for r in range(2):
            add_terms(blocks_ref, index_ref, partial_ref, t, r, wide_column(columns, t, r))


def total_of(pieces_ref):
    total = pieces_ref[0]
    for p in range(1, PEERS):
        total = total + pieces_ref[p]
    return total


def to_all(ref, value, count):
    for p in range(count):
        ref[p] = value


def tile_of(tile, pieces_ref, cost_ref):
    tile[0:PIECE, :] = total_of(pieces_ref)
    own = pl.multiple_of(lax.axis_index(TWIN) * 16, 16)
    tile[pl.ds(own, 8), :] -= cost_ref[:, :128]
    tile[pl.ds(own + 8, 8), :] -= cost_ref[:, 128:]


def sum_first(pieces_ref, cost_ref, primal_ref, tiles_ref, tile):
    tile_of(tile, pieces_ref, cost_ref)
    tile[40:48, :] = primal_ref[:, :128]
    tile[48:56, :] = primal_ref[:, 128:]
    to_all(tiles_ref, tile[...], LINE_PEERS)


def sum_second(pieces_ref, cost_ref, tiles_ref, tile):
    tile_of(tile, pieces_ref, cost_ref)
    to_all(tiles_ref, tile[...], LINE_PEERS)


def for_other_core(tiles_ref, pack_ref):
    chip = lax.axis_index("section_0")
    core = lax.axis_index(CORE)
    above = 2 * jnp.minimum(chip + 1 - core, 3)
    below = 2 * jnp.maximum(chip - core, 0)
    last = pl.ds(7, 4, stride=8)
    pack_ref[...] = jnp.zeros_like(pack_ref)
    pack_ref[0:4, :] = tiles_ref[above, HALO] + tiles_ref[above + 1, HALO]
    pack_ref[4:8, :] = tiles_ref[below, last] + tiles_ref[below + 1, last]
    if tiles_ref.shape[1] > PIECE:
        late = pl.ds(47, 2, stride=8)
        pack_ref[8:10, :] = tiles_ref[below, late]
        pack_ref[10:12, :] = tiles_ref[below + 1, late]
    moves = tiles_ref[0, 36:40]
    for d in range(1, LINE_PEERS):
        moves = moves + tiles_ref[d, 36:40]
    pack_ref[12:16, :] = moves


def descents(tiles_ref, other_ref, descent):
    section = lax.axis_index(SECTION)
    here = 2 * lax.axis_index("section_0")
    descent[...] = tiles_ref[here, 0:CHUNK] + tiles_ref[here + 1, 0:CHUNK]
    descent[pl.ds(7, 4, stride=8), :] += jnp.where(section < 7, other_ref[0:4], 0.0)
    before = other_ref[4:8] + tiles_ref[here, HALO] + tiles_ref[here + 1, HALO]
    return descent[...], before


def send_field(copies_ref, field, before):
    to_all(copies_ref, jnp.concatenate([field, before, jnp.zeros((4, 128), f32)], 0), PEERS)


def primal_step(
    weight_ref, tiles_ref, other_ref, copies_ref, primal_one_ref, before_one_ref, move_ref, descent
):
    tau = step_scale / jnp.full((1, 128), weight_ref[0], f32)
    along, along_before = descents(tiles_ref, other_ref, descent)
    here = 2 * lax.axis_index("section_0")
    start = jnp.concatenate([tiles_ref[here, 40:56], tiles_ref[here + 1, 40:56]], 0)
    start_before = other_ref[8:12]
    primal_one = jnp.maximum(0.0, start + tau * along)
    before_one = jnp.maximum(0.0, start_before + tau * along_before)
    primal_one_ref[...] = primal_one
    before_one_ref[...] = before_one
    move_ref[...] = 0.5 * jnp.sum((primal_one - start) ** 2, axis=0, keepdims=True)
    send_field(copies_ref, 2.0 * primal_one - start, 2.0 * before_one - start_before)


def dual_step(
    index_ref, weight_ref, blocks_ref, field_ref, dual_ref, demand_ref, move_x, dual_one_ref, partial_ref
):
    partial_ref[...] = jnp.zeros_like(partial_ref)
    sigma = step_scale * weight_ref[0]
    start = columns_of(dual_ref)
    demand = columns_of(demand_ref)
    product = all_products(blocks_ref, index_ref, field_ref)
    dual_one = start + sigma * (demand - product)
    for t in range(PERIODS_HERE):
        for r in range(2):
            add_terms(blocks_ref, index_ref, partial_ref, t, r, wide_column(dual_one, t, r))
    move = jnp.sum((dual_one - start).T ** 2, axis=0, keepdims=True)
    moves = jnp.concatenate([move_x[...], move], 0)
    for p in range(PEERS):
        partial_ref[p * PIECE + 36 : p * PIECE + 38, :] = moves
    store_rows(dual_one_ref, dual_one.T)


def primal_last(
    weight_ref, tiles_ref, other_ref, primal_one_ref, before_one_ref, copies_ref, primal_ref, steps_ref, descent
):
    moves = other_ref[8:16]
    for d in range(LINE_PEERS):
        moves = moves + tiles_ref[d, 32:40]
    move = jnp.broadcast_to(jnp.sum(moves, axis=1, keepdims=True), (8, 128))
    move_primal, move_dual = move[4:5], move[5:6]
    weight = jnp.full((1, 128), weight_ref[0], f32)
    omega = jnp.sqrt(weight * jnp.sqrt((move_dual + epsilon) / (move_primal + epsilon)))
    tau = step_scale / omega
    steps_ref[...] = jnp.broadcast_to(step_scale * omega, (8, 128))
    along, along_before = descents(tiles_ref, other_ref, descent)
    primal_one = primal_one_ref[...]
    before_one = before_one_ref[...]
    primal = jnp.maximum(0.0, primal_one + tau * along)
    before = jnp.maximum(0.0, before_one + tau * along_before)
    primal_ref[...] = primal
    send_field(copies_ref, 2.0 * primal - primal_one, 2.0 * before - before_one)


def dual_last(
    index_ref, blocks_ref, field_ref, steps_ref, dual_ref, demand_ref, primal_ref, primal_out, dual_out
):
    own = pl.multiple_of(lax.axis_index(TWIN) * 16, 16)
    primal_out[:, :128] = primal_ref[pl.ds(own, 8), :]
    primal_out[:, 128:] = primal_ref[pl.ds(own + 8, 8), :]
    result = all_products(blocks_ref, index_ref, field_ref).T
    sigma = steps_ref[...]
    for r in range(2):
        part = slice(r * 128, r * 128 + 128)
        dual_out[:, part] = dual_ref[:, part] + sigma * (
            demand_ref[:, part] - result[r * 8 : r * 8 + 8]
        )


def to_other_core(x):
    return lax.ppermute(x, CORE, [(0, 1), (1, 0)])


def exchange(pieces, axis):
    return lax.all_to_all(pieces, axis, split_axis=0, concat_axis=0, tiled=True)


def in_hbm(x):
    return pltpu.with_memory_space_constraint(x, pltpu.HBM)


def on_device(
    blocks, column_index, block_period, cost_vector, demand, primal_start, dual_start, primal_weight
):
    partials = shaped(PEERS * PIECE, 128)
    pieces = (PEERS, PIECE, 128)
    chunk = shaped(CHUNK, 128)
    local = shaped(8, 256)
    pack = shaped(16, 128)
    rows = pltpu.VMEM((CHUNK, 128), f32)

    index, partial, kept = call(
        adjoint_start,
        [jax.ShapeDtypeStruct((96,), jnp.int32), partials, shaped(*blocks.shape)],
        [HBM] * 4,
        [
            pltpu.SMEM((6, 2, 8), jnp.int32),
            pltpu.SMEM((6, 2, 8), jnp.int32),
            pltpu.VMEM((8, 256), f32),
            pltpu.SemaphoreType.DMA((11,)),
        ],
        [SMEM, VMEM, VMEM],
    )(
        in_hbm(column_index.transpose(2, 1, 0)),
        in_hbm(block_period.transpose(2, 1, 0)),
        in_hbm(blocks),
        in_hbm(dual_start),
    )
    kept = pltpu.with_memory_space_constraint(kept, pltpu.VMEM)
    arrived = exchange(partial.reshape(pieces), PLANE)
    tiles = call(
        sum_first, shaped(LINE_PEERS, 56, 128), [VMEM] * 3, [pltpu.VMEM((56, 128), f32)]
    )(arrived, cost_vector, primal_start)
    tiles = exchange(tiles, LINE)
    other = to_other_core(call(for_other_core, pack, [VMEM])(tiles))
    send, primal_one, before_one, move_primal = call(
        primal_step,
        [shaped(*pieces), chunk, shaped(4, 128), shaped(1, 128)],
        [SMEM, VMEM, VMEM],
        [rows],
    )(primal_weight, tiles, other)
    field = exchange(send, PLANE).reshape(PEERS * PIECE, 128)
    dual_one, partial = call(dual_step, [local, partials], [SMEM, SMEM] + [VMEM] * 5)(
        index, primal_weight, kept, field, dual_start, demand, move_primal
    )
    arrived = exchange(partial.reshape(pieces), PLANE)
    tiles = call(sum_second, shaped(LINE_PEERS, PIECE, 128), [VMEM] * 2, [pltpu.VMEM((PIECE, 128), f32)])(
        arrived, cost_vector
    )
    tiles = exchange(tiles, LINE)
    other = to_other_core(call(for_other_core, pack, [VMEM])(tiles))
    send, primal, steps = call(
        primal_last, [shaped(*pieces), chunk, shaped(8, 128)], [SMEM] + [VMEM] * 4, [rows]
    )(primal_weight, tiles, other, primal_one, before_one)
    field = exchange(send, PLANE).reshape(PEERS * PIECE, 128)
    primal_final, dual_final = call(dual_last, [local, local], [SMEM] + [VMEM] * 6)(
        index, kept, field, steps, dual_one, demand, primal
    )
    return primal_final, dual_final


def solution(mesh):
    finer = Mesh(mesh.devices.reshape(4, 2, 4, 2, 4), AXES)
    return jax.shard_map(
        on_device,
        mesh=finer,
        in_specs=(
            P(SECTION, DOM, None, None, None),
            P(SECTION, DOM, None),
            P(SECTION, DOM, None),
            P(SECTION, DOM),
            P(SECTION, DOM),
            P(SECTION, DOM),
            P(SECTION, DOM),
            P(),
        ),
        out_specs=(P(SECTION, DOM), P(SECTION, DOM)),
        check_vma=False,
    )
```

time: 173 us -> 92.2 us (0.53)
  starting transfers between devices: 40.6 us -> 7.95 us
  matrix products: 25.4 us -> 0 us
  waiting for transfers between devices: 18.6 us -> 1.01 us
  Pallas kernels: 0 us -> 7.15 us
  other arithmetic: 6.8 us -> 0 us
  local copies, waits for them, and re-layouts: 3.65 us -> 0.02 us
    psum x5 -> x0, blocking collectives: 40.6 us -> none  [by_axis(): return functools.reduce(lax.psum, axes, x)]
    all_to_all x2 -> x6, blocking collectives: 33.9 us -> 74.4 us  [exchange(): return lax.all_to_all(pieces, axis, split_axis=0, concat_axis=0, tiled=True)]
    dot_general x4 -> x0, matrix products: 25.4 us -> none  [the longest x2 14.2 us: forward(): jnp.einsum('prkij,prkj->pri', blocks, picked, precision=lax.Precision.HIG...]
    all_to_all x2 -> x0, starting transfers between devices: 17.1 us -> none  [summed_on_arrival(): lax.all_to_all(pieces, axis, split_axis=0, concat_axis=0, tiled=True)]
    ppermute x4 -> x2, starting transfers between devices: 23.5 us -> 7.95 us  [to_other_core(): return lax.ppermute(x, CORE, [(0, 1), (1, 0)])]
    all_to_all x2 -> x0, waiting for transfers between devices: 12.1 us -> none  [summed_on_arrival(): lax.all_to_all(pieces, axis, split_axis=0, concat_axis=0, tiled=True)]
    pallas_call x0 -> x9, Pallas kernels: none -> 7.15 us  [the longest x1 3.5 us: on_device(): call(adjoint_start, [jax.ShapeDtypeStruct((96,), jnp.int32), partials, sh...]
    ppermute x4 -> x2, waiting for transfers between devices: 6.48 us -> 1.01 us  [to_other_core(): return lax.ppermute(x, CORE, [(0, 1), (1, 0)])]
  transfers between devices with their start and end apart: 6 -> 2, of which waited for: 5 -> 2; matrix products, arithmetic and copies ran while one was open for 0% -> 0% of each run, Pallas kernels for 0% -> 0%
where the time goes in v3:
time: 92.2 us; the launch traced here: 91.9 us
  blocking collectives  74.4 us (81%)
  starting transfers between devices  7.95 us (9%)
  Pallas kernels  7.15 us (8%)
  between operations  1.35 us (1%)
  waiting for transfers between devices  1.01 us (1%)
    all_to_all x6, blocking collectives, exchange(): return lax.all_to_all(pieces, axis, split_axis=0, concat_axis=0, tiled=True)  74.4 us
    ppermute x2, starting transfers between devices, to_other_core(): return lax.ppermute(x, CORE, [(0, 1), (1, 0)])  7.95 us
    pallas_call x1, Pallas kernels, on_device(): call(adjoint_start, [jax.ShapeDtypeStruct((96,), jnp.int32), partials, sh...  3.5 us
  transfers between devices with their start and end apart: 2, of which 2 were waited for; matrix products, arithmetic and copies ran while one was open for 0% of the time, Pallas kernels for 0%

profile of v3, /device:TPU:1, one launch (start us, length us, event | category | flops | bytes accessed | tf_op | source)
XLA Modules:
  0.0 91.9 jit_solution(12791855104549880606)
XLA Ops:
  0.6 0.0 copy-start
  0.6 0.0 copy-start.1
  0.7 0.0 copy-start.3
  0.7 0.0 copy-start.2
  0.7 3.5 %shard_map.95 = (s32[96]{0:T(128)S(1)}, f32[640,128]{1,0:T(8,128)S(1)}, f32[8,2,6,128,128]{4,3,2,1,0:T(8,128)S(1)}) custom-call(s32[6,2,8]{2,1,0:T(2,128)} %bitcast.10, s32[6,2,8]{2,1,0:T(2,128)} %bitcast.11, f32[8,2,6,128,128]{4,3,2,1,0:T(8,128)} %blocks_in.1, f32[8,256]{1,0:T(8,128)} %dual_ref.1), custom_call_target="tpu_custom_call" | custom-call | tf_op jit(solution)/shard_map/pallas_call | solution.py:281
  4.2 15.9 %all_to_all.30.pieces_ref = f32[16,40,128]{2,1,0:T(8,128)S(1)} all-to-all(f32[16,40,128]{2,1,0:T(8,128)S(1)} %bitcast.9), channel_id=1, replica_groups=mesh['section_0'=4,'section_1'=2,'dom_0'=4,'dom_1'=2,'dom_2'=4] {'dom_0'..., dimensions={0} | all-to-all | bytes 655360 | tf_op jit(solution)/shard_map/all_to_all | solution.py:264
  20.0 0.0 copy-done.1
  20.0 0.0 copy-done.3
  20.1 15.0 %all_to_all.31.tiles_ref = f32[8,56,128]{2,1,0:T(8,128)S(1)} all-to-all(f32[8,56,128]{2,1,0:T(8,128)S(1)} %shard_map.96), channel_id=1, replica_groups=mesh['section_0'=4,'section_1'=2,'dom_0'=4,'dom_1'=2,'dom_2'=4] {'sectio..., dimensions={0} | all-to-all | bytes 458752 | tf_op jit(solution)/shard_map/all_to_all | solution.py:264
  35.1 3.8 %collective-permute-start = (f32[16,128]{1,0:T(8,128)S(1)}, f32[16,128]{1,0:T(8,128)S(1)}, u32[]{:S(2)}, u32[]{:S(2)}) collective-permute-start(f32[16,128]{1,0:T(8,128)S(1)} %shard_map.97), channel_id=1, source_target_pairs={{0,32},{32,0},{1,33},{33,1},{2,34},{34,2},{3,35},{35,3},{4,36},{36... | collective-permute-start | bytes 24584 | tf_op jit(solution)/shard_map/ppermute | solution.py:260
  39.6 0.2 collective-permute-done.other_ref
  39.8 11.7 %all_to_all.32 = f32[16,40,128]{2,1,0:T(8,128)S(1)} all-to-all(f32[16,40,128]{2,1,0:T(8,128)S(1)} %get-tuple-element.17), channel_id=1, replica_groups=mesh['section_0'=4,'section_1'=2,'dom_0'=4,'dom_1'=2,'dom_2'=4] {'dom_0'..., dimensions={0} | all-to-all | bytes 655360 | tf_op jit(solution)/shard_map/all_to_all | solution.py:264
  51.4 0.0 copy-done
  51.4 0.0 copy-done.2
  51.4 1.7 %shard_map.99 = (f32[8,256]{1,0:T(8,128)S(1)}, f32[640,128]{1,0:T(8,128)S(1)}) custom-call(s32[96]{0:T(128)S(1)} %get-tuple-element.14.index_ref, f32[1]{0:T(128)S(6)} %copy.10.weight_ref, f32[8,2,6,128,128]{4,3,2,1,0:T(8,128)S(1)} %get-tuple-element.15.blocks_ref, f32[640,128]{1,0:T(8,128)S(1)} %bitcast.7, f32[8,256]{1,0:T(8,128)S(1)} %copy-done, ...), custom_call_target="tpu_custom_call" | custom-call | tf_op jit(solution)/shard_map/pallas_call | solution.py:312
  53.1 10.6 %all_to_all.33.pieces_ref = f32[16,40,128]{2,1,0:T(8,128)S(1)} all-to-all(f32[16,40,128]{2,1,0:T(8,128)S(1)} %bitcast.8), channel_id=1, replica_groups=mesh['section_0'=4,'section_1'=2,'dom_0'=4,'dom_1'=2,'dom_2'=4] {'dom_0'..., dimensions={0} | all-to-all | bytes 655360 | tf_op jit(solution)/shard_map/all_to_all | solution.py:264
  63.8 9.6 %all_to_all.34.tiles_ref = f32[8,40,128]{2,1,0:T(8,128)S(1)} all-to-all(f32[8,40,128]{2,1,0:T(8,128)S(1)} %shard_map.100), channel_id=1, replica_groups=mesh['section_0'=4,'section_1'=2,'dom_0'=4,'dom_1'=2,'dom_2'=4] {'sectio..., dimensions={0} | all-to-all | bytes 327680 | tf_op jit(solution)/shard_map/all_to_all | solution.py:264
  73.4 4.1 %collective-permute-start.1 = (f32[16,128]{1,0:T(8,128)S(1)}, f32[16,128]{1,0:T(8,128)S(1)}, u32[]{:S(2)}, u32[]{:S(2)}) collective-permute-start(f32[16,128]{1,0:T(8,128)S(1)} %shard_map.101), channel_id=1, source_target_pairs={{0,32},{32,0},{1,33},{33,1},{2,34},{34,2},{3,35},{35,3},{4,36},{36... | collective-permute-start | bytes 24584 | tf_op jit(solution)/shard_map/ppermute | solution.py:260
  77.6 0.8 collective-permute-done.1.other_ref
  78.4 0.1 shard_map.102
  78.5 11.6 %all_to_all.35 = f32[16,40,128]{2,1,0:T(8,128)S(1)} all-to-all(f32[16,40,128]{2,1,0:T(8,128)S(1)} %get-tuple-element.22), channel_id=1, replica_groups=mesh['section_0'=4,'section_1'=2,'dom_0'=4,'dom_1'=2,'dom_2'=4] {'dom_0'..., dimensions={0} | all-to-all | bytes 655360 | tf_op jit(solution)/shard_map/all_to_all | solution.py:264
  90.2 1.7 %shard_map.103 = (f32[8,256]{1,0:T(8,128)}, f32[8,256]{1,0:T(8,128)}) custom-call(s32[96]{0:T(128)S(1)} %get-tuple-element.14.index_ref, f32[8,2,6,128,128]{4,3,2,1,0:T(8,128)S(1)} %get-tuple-element.15.blocks_ref, f32[640,128]{1,0:T(8,128)S(1)} %bitcast.6, f32[8,128]{1,0:T(8,128)S(1)} %get-tuple-element.23.steps_ref, ...), custom_call_target="tpu_custom_call" | custom-call | tf_op jit(solution)/shard_map/pallas_call | solution.py:325
  (5 shorter events, 0.1 us)
Async XLA Ops:
  0.6 50.8 %copy-start = (f32[8,256]{1,0:T(8,128)S(1)}, f32[8,256]{1,0:T(8,128)}, u32[]{:S(2)}) copy-start(f32[8,256]{1,0:T(8,128)} %dual_ref.1) | copy-start | bytes 24580
  0.6 19.4 %copy-start.1 = (f32[8,256]{1,0:T(8,128)S(1)}, f32[8,256]{1,0:T(8,128)}, u32[]{:S(2)}) copy-start(f32[8,256]{1,0:T(8,128)} %cost_ref.3) | copy-start | bytes 24580
  0.7 19.4 %copy-start.3 = (f32[8,256]{1,0:T(8,128)S(1)}, f32[8,256]{1,0:T(8,128)}, u32[]{:S(2)}) copy-start(f32[8,256]{1,0:T(8,128)} %primal_ref.1) | copy-start | bytes 24580
  0.7 50.8 %copy-start.2 = (f32[8,256]{1,0:T(8,128)S(1)}, f32[8,256]{1,0:T(8,128)}, u32[]{:S(2)}) copy-start(f32[8,256]{1,0:T(8,128)} %demand_ref.3) | copy-start | bytes 24580
  35.1 4.7 %collective-permute-start = (f32[16,128]{1,0:T(8,128)S(1)}, f32[16,128]{1,0:T(8,128)S(1)}, u32[]{:S(2)}, u32[]{:S(2)}) collective-permute-start(f32[16,128]{1,0:T(8,128)S(1)} %shard_map.97), channel_id=1, source_target_pairs={{0,32},{32,0},{1,33},{33,1},{2,34},{34,2},{3,35},{35,3},{4,36},{36... | collective-permute-start | bytes 24584 | tf_op jit(solution)/shard_map/ppermute | solution.py:260
  73.4 5.0 %collective-permute-start.1 = (f32[16,128]{1,0:T(8,128)S(1)}, f32[16,128]{1,0:T(8,128)S(1)}, u32[]{:S(2)}, u32[]{:S(2)}) collective-permute-start(f32[16,128]{1,0:T(8,128)S(1)} %shard_map.101), channel_id=1, source_target_pairs={{0,32},{32,0},{1,33},{33,1},{2,34},{34,2},{3,35},{35,3},{4,36},{36... | collective-permute-start | bytes 24584 | tf_op jit(solution)/shard_map/ppermute | solution.py:260

commit v4 on v3

--- a/solution.py
+++ b/solution.py
@@ -37,12 +37,12 @@
     return jax.ShapeDtypeStruct(shape, f32)
 
 
-def call(kernel, outs, ins, scratch=(), places=None):
+def call(kernel, outs, ins, scratch=()):
     return pl.pallas_call(
         kernel,
         out_shape=outs,
         in_specs=ins,
-        out_specs=places or jax.tree.map(lambda _: VMEM, outs),
+        out_specs=jax.tree.map(lambda _: VMEM, outs),
         scratch_shapes=list(scratch),
         compiler_params=PARAMS,
     )
@@ -86,9 +86,22 @@
     return jnp.broadcast_to(columns[:, place : place + 1], (128, 128))
 
 
+def fill_index(column_ref, period_ref, index_ref, t):
+    for r in range(2):
+        for k in range(6):
+            c = column_ref[k, r, t]
+            before = lax.axis_index(SECTION) * PERIODS_HERE + t - period_ref[k, r, t]
+            peer = (c >> 4) * 4 + ((c >> 1) & 3)
+            inside = ((c >> 3) & 1) * 2 + (c & 1)
+            row = inside * 8 + t - before
+            if t == 0:
+                row = jnp.where(before == 0, inside * 8, inside + CHUNK)
+            index_ref[t * 12 + r * 6 + k] = peer * PIECE + row
+
+
 def adjoint_start(
-    column_in, period_in, blocks_in, dual_in, index_ref, partial_ref, blocks_ref,
-    column_ref, period_ref, dual_ref, arrived,
+    column_in, period_in, blocks_in, dual_in, index_out, partial_ref, blocks_ref,
+    column_ref, period_ref, index_ref, dual_ref, arrived,
 ):
     get_column = pltpu.make_async_copy(column_in, column_ref, arrived.at[0])
     get_period = pltpu.make_async_copy(period_in, period_ref, arrived.at[1])
@@ -100,26 +113,19 @@
     for copy in [get_column, get_period, get_dual] + get_blocks:
         copy.start()
     partial_ref[...] = jnp.zeros_like(partial_ref)
-    first_period = lax.axis_index(SECTION) * PERIODS_HERE
+    get_dual.wait()
+    columns = columns_of(dual_ref)
     get_column.wait()
     get_period.wait()
     for t in range(PERIODS_HERE):
-        for r in range(2):
-            for k in range(6):
-                c = column_ref[k, r, t]
-                before = first_period + t - period_ref[k, r, t]
-                peer = (c >> 4) * 4 + ((c >> 1) & 3)
-                inside = ((c >> 3) & 1) * 2 + (c & 1)
-                row = inside * 8 + t - before
-                if t == 0:
-                    row = jnp.where(before == 0, inside * 8, inside + CHUNK)
-                index_ref[t * 12 + r * 6 + k] = peer * PIECE + row
-    get_dual.wait()
-    columns = columns_of(dual_ref)
+        fill_index(column_ref, period_ref, index_ref, t)
+    put_index = pltpu.make_async_copy(index_ref, index_out, arrived.at[11])
+    put_index.start()
     for t in range(PERIODS_HERE):
         get_blocks[t].wait()
         for r in range(2):
             add_terms(blocks_ref, index_ref, partial_ref, t, r, wide_column(columns, t, r))
+    put_index.wait()
 
 
 def total_of(pieces_ref):
@@ -143,8 +149,8 @@
 
 def sum_first(pieces_ref, cost_ref, primal_ref, tiles_ref, tile):
     tile_of(tile, pieces_ref, cost_ref)
-    tile[40:48, :] = primal_ref[:, :128]
-    tile[48:56, :] = primal_ref[:, 128:]
+    tile[36:37, :] = primal_ref[7:8, :128]
+    tile[37:38, :] = primal_ref[7:8, 128:]
     to_all(tiles_ref, tile[...], LINE_PEERS)
 
 
@@ -162,10 +168,8 @@
     pack_ref[...] = jnp.zeros_like(pack_ref)
     pack_ref[0:4, :] = tiles_ref[above, HALO] + tiles_ref[above + 1, HALO]
     pack_ref[4:8, :] = tiles_ref[below, last] + tiles_ref[below + 1, last]
-    if tiles_ref.shape[1] > PIECE:
-        late = pl.ds(47, 2, stride=8)
-        pack_ref[8:10, :] = tiles_ref[below, late]
-        pack_ref[10:12, :] = tiles_ref[below + 1, late]
+    pack_ref[8:10, :] = tiles_ref[below, 36:38]
+    pack_ref[10:12, :] = tiles_ref[below + 1, 36:38]
     moves = tiles_ref[0, 36:40]
     for d in range(1, LINE_PEERS):
         moves = moves + tiles_ref[d, 36:40]
@@ -186,12 +190,16 @@
 
 
 def primal_step(
-    weight_ref, tiles_ref, other_ref, copies_ref, primal_one_ref, before_one_ref, move_ref, descent
+    weight_ref, tiles_ref, other_ref, primal_ref, twin_ref, copies_ref, primal_one_ref, before_one_ref, move_ref,
+    descent,
 ):
     tau = step_scale / jnp.full((1, 128), weight_ref[0], f32)
     along, along_before = descents(tiles_ref, other_ref, descent)
-    here = 2 * lax.axis_index("section_0")
-    start = jnp.concatenate([tiles_ref[here, 40:56], tiles_ref[here + 1, 40:56]], 0)
+    first = lax.axis_index(TWIN) == 0
+    own, twin = (
+        jnp.concatenate([ref[:, :128], ref[:, 128:]], 0) for ref in (primal_ref, twin_ref)
+    )
+    start = jnp.concatenate([jnp.where(first, own, twin), jnp.where(first, twin, own)], 0)
     start_before = other_ref[8:12]
     primal_one = jnp.maximum(0.0, start + tau * along)
     before_one = jnp.maximum(0.0, start_before + tau * along_before)
@@ -202,12 +210,16 @@
 
 
 def dual_step(
-    index_ref, weight_ref, blocks_ref, field_ref, dual_ref, demand_ref, move_x, dual_one_ref, partial_ref
-):
+    index_in, weight_ref, blocks_ref, field_ref, dual_ref, demand_ref, move_x, dual_one_ref, partial_ref,
+    index_ref, arrived,
+):
+    get_index = pltpu.make_async_copy(index_in, index_ref, arrived)
+    get_index.start()
     partial_ref[...] = jnp.zeros_like(partial_ref)
     sigma = step_scale * weight_ref[0]
     start = columns_of(dual_ref)
     demand = columns_of(demand_ref)
+    get_index.wait()
     product = all_products(blocks_ref, index_ref, field_ref)
     dual_one = start + sigma * (demand - product)
     for t in range(PERIODS_HERE):
@@ -242,11 +254,15 @@
 
 
 def dual_last(
-    index_ref, blocks_ref, field_ref, steps_ref, dual_ref, demand_ref, primal_ref, primal_out, dual_out
-):
+    index_in, blocks_ref, field_ref, steps_ref, dual_ref, demand_ref, primal_ref, primal_out, dual_out,
+    index_ref, arrived,
+):
+    get_index = pltpu.make_async_copy(index_in, index_ref, arrived)
+    get_index.start()
     own = pl.multiple_of(lax.axis_index(TWIN) * 16, 16)
     primal_out[:, :128] = primal_ref[pl.ds(own, 8), :]
     primal_out[:, 128:] = primal_ref[pl.ds(own + 8, 8), :]
+    get_index.wait()
     result = all_products(blocks_ref, index_ref, field_ref).T
     sigma = steps_ref[...]
     for r in range(2):
@@ -277,7 +293,11 @@
     local = shaped(8, 256)
     pack = shaped(16, 128)
     rows = pltpu.VMEM((CHUNK, 128), f32)
-
+    tile = shaped(LINE_PEERS, PIECE, 128)
+    rows_of_tile = [pltpu.VMEM((PIECE, 128), f32)]
+    primal_twin = lax.ppermute(primal_start, TWIN, [(0, 1), (1, 0)])
+
+    places = [pltpu.SMEM((96,), jnp.int32), pltpu.SemaphoreType.DMA(())]
     index, partial, kept = call(
         adjoint_start,
         [jax.ShapeDtypeStruct((96,), jnp.int32), partials, shaped(*blocks.shape)],
@@ -285,10 +305,10 @@
         [
             pltpu.SMEM((6, 2, 8), jnp.int32),
             pltpu.SMEM((6, 2, 8), jnp.int32),
+            places[0],
             pltpu.VMEM((8, 256), f32),
-            pltpu.SemaphoreType.DMA((11,)),
+            pltpu.SemaphoreType.DMA((12,)),
         ],
-        [SMEM, VMEM, VMEM],
     )(
         in_hbm(column_index.transpose(2, 1, 0)),
         in_hbm(block_period.transpose(2, 1, 0)),
@@ -297,32 +317,30 @@
     )
     kept = pltpu.with_memory_space_constraint(kept, pltpu.VMEM)
     arrived = exchange(partial.reshape(pieces), PLANE)
-    tiles = call(
-        sum_first, shaped(LINE_PEERS, 56, 128), [VMEM] * 3, [pltpu.VMEM((56, 128), f32)]
-    )(arrived, cost_vector, primal_start)
+    tiles = call(sum_first, tile, [VMEM] * 3, rows_of_tile)(arrived, cost_vector, primal_start)
     tiles = exchange(tiles, LINE)
     other = to_other_core(call(for_other_core, pack, [VMEM])(tiles))
     send, primal_one, before_one, move_primal = call(
         primal_step,
         [shaped(*pieces), chunk, shaped(4, 128), shaped(1, 128)],
-        [SMEM, VMEM, VMEM],
+        [SMEM] + [VMEM] * 4,
         [rows],
-    )(primal_weight, tiles, other)
+    )(primal_weight, tiles, other, primal_start, primal_twin)
     field = exchange(send, PLANE).reshape(PEERS * PIECE, 128)
-    dual_one, partial = call(dual_step, [local, partials], [SMEM, SMEM] + [VMEM] * 5)(
+    dual_one, partial = call(
+        dual_step, [local, partials], [VMEM, SMEM] + [VMEM] * 5, places
+    )(
         index, primal_weight, kept, field, dual_start, demand, move_primal
     )
     arrived = exchange(partial.reshape(pieces), PLANE)
-    tiles = call(sum_second, shaped(LINE_PEERS, PIECE, 128), [VMEM] * 2, [pltpu.VMEM((PIECE, 128), f32)])(
-        arrived, cost_vector
-    )
+    tiles = call(sum_second, tile, [VMEM] * 2, rows_of_tile)(arrived, cost_vector)
     tiles = exchange(tiles, LINE)
     other = to_other_core(call(for_other_core, pack, [VMEM])(tiles))
     send, primal, steps = call(
         primal_last, [shaped(*pieces), chunk, shaped(8, 128)], [SMEM] + [VMEM] * 4, [rows]
     )(primal_weight, tiles, other, primal_one, before_one)
     field = exchange(send, PLANE).reshape(PEERS * PIECE, 128)
-    primal_final, dual_final = call(dual_last, [local, local], [SMEM] + [VMEM] * 6)(
+    primal_final, dual_final = call(dual_last, [local, local], [VMEM] * 7, places)(
         index, kept, field, steps, dual_one, demand, primal
     )
     return primal_final, dual_final

time: 92.2 us -> 99.2 us (1.076)
  blocking collectives: 74.4 us -> 59.3 us
  starting transfers between devices: 7.95 us -> 22.8 us
  local copies, waits for them, and re-layouts: 0.02 us -> 5.45 us
  waiting for transfers between devices: 1.01 us -> 2.51 us
    all_to_all x6 -> x5, blocking collectives: 74.4 us -> 59.3 us  [exchange(): return lax.all_to_all(pieces, axis, split_axis=0, concat_axis=0, tiled=True)]
    all_to_all x0 -> x1, starting transfers between devices: none -> 8.18 us  [exchange(): return lax.all_to_all(pieces, axis, split_axis=0, concat_axis=0, tiled=True)]
    unnamed x8 -> x14, local copies, waits for them, and re-layouts: 0.02 us -> 5.45 us
    ppermute x0 -> x1, starting transfers between devices: none -> 5.37 us  [on_device(): primal_twin = lax.ppermute(primal_start, TWIN, [(0, 1), (1, 0)])]
    all_to_all x0 -> x1, waiting for transfers between devices: none -> 1.51 us  [exchange(): return lax.all_to_all(pieces, axis, split_axis=0, concat_axis=0, tiled=True)]
    ppermute x2, starting transfers between devices: 7.95 us -> 9.25 us  [to_other_core(): return lax.ppermute(x, CORE, [(0, 1), (1, 0)])]
  transfers between devices with their start and end apart: 2 -> 4, of which waited for: 2 -> 3; matrix products, arithmetic and copies ran while one was open for 0% -> 0% of each run, Pallas kernels for 0% -> 0%
where the time goes in v4:
time: 99.2 us; the launch traced here: 98.9 us
  blocking collectives  59.3 us (60%)
  starting transfers between devices  22.8 us (23%)
  Pallas kernels  7.47 us (8%)
  local copies, waits for them, and re-layouts  5.45 us (5%)
  waiting for transfers between devices  2.51 us (3%)
  between operations  1.38 us (1%)
    all_to_all x5, blocking collectives, exchange(): return lax.all_to_all(pieces, axis, split_axis=0, concat_axis=0, tiled=True)  59.3 us
    ppermute x2, starting transfers between devices, to_other_core(): return lax.ppermute(x, CORE, [(0, 1), (1, 0)])  9.25 us
    all_to_all x1, starting transfers between devices, exchange(): return lax.all_to_all(pieces, axis, split_axis=0, concat_axis=0, tiled=True)  8.18 us
    unnamed x14, local copies, waits for them, and re-layouts  5.45 us
    ppermute x1, starting transfers between devices, on_device(): primal_twin = lax.ppermute(primal_start, TWIN, [(0, 1), (1, 0)])  5.37 us
    pallas_call x1, Pallas kernels, on_device(): call(adjoint_start, [jax.ShapeDtypeStruct((96,), jnp.int32), partials, sh...  3.07 us
  transfers between devices with their start and end apart: 4, of which 3 were waited for; matrix products, arithmetic and copies ran while one was open for 0% of the time, Pallas kernels for 0%

profile of v4, /device:TPU:1, one launch (start us, length us, event | category | flops | bytes accessed | tf_op | source)
XLA Modules:
  0.0 98.9 jit_solution(17101844677101625334)
XLA Ops:
  0.6 0.0 copy-start.3
  0.6 0.0 copy-start.6
  0.7 0.0 copy-start.4
  0.7 0.0 copy-start.5
  0.7 3.1 %shard_map.95 = (s32[96]{0:T(128)S(1)}, f32[640,128]{1,0:T(8,128)S(1)}, f32[8,2,6,128,128]{4,3,2,1,0:T(8,128)S(1)}) custom-call(s32[6,2,8]{2,1,0:T(2,128)} %bitcast.10, s32[6,2,8]{2,1,0:T(2,128)} %bitcast.11, f32[8,2,6,128,128]{4,3,2,1,0:T(8,128)} %blocks_in.1, f32[8,256]{1,0:T(8,128)} %dual_ref.1), custom_call_target="tpu_custom_call" | custom-call | tf_op jit(solution)/shard_map/pallas_call | solution.py:301
  3.7 0.0 copy-start
  3.8 2.6 %copy-done = f32[8,2,6,128,128]{4,3,2,1,0:T(8,128)} copy-done((f32[8,2,6,128,128]{4,3,2,1,0:T(8,128)}, f32[8,2,6,128,128]{4,3,2,1,0:T(8,128)S(1)}, u32[]{:S(2)}) %copy-start) | copy-done | bytes 6291480
  6.4 15.8 %all_to_all.30.pieces_ref = f32[16,40,128]{2,1,0:T(8,128)S(1)} all-to-all(f32[16,40,128]{2,1,0:T(8,128)S(1)} %bitcast.9), channel_id=1, replica_groups=mesh['section_0'=4,'section_1'=2,'dom_0'=4,'dom_1'=2,'dom_2'=4] {'dom_0'..., dimensions={0} | all-to-all | bytes 655360 | tf_op jit(solution)/shard_map/all_to_all | solution.py:280
  22.2 0.0 copy-done.6
  22.3 0.0 copy-done.4
  22.3 0.7 shard_map.96
  23.0 8.2 %all-to-all-start.1 = ((f32[8,40,128]{2,1,0:T(8,128)}), f32[8,40,128]{2,1,0:T(8,128)S(1)}, u32[]{:S(2)}, u32[]{:S(2)}) async-start(f32[8,40,128]{2,1,0:T(8,128)} %shard_map.96), calls=%async_computation.1 | async-start | bytes 327680 | tf_op jit(solution)/shard_map/all_to_all | solution.py:280
  31.1 5.4 %collective-permute-start.1 = (f32[8,256]{1,0:T(8,128)S(1)}, f32[8,256]{1,0:T(8,128)S(1)}, u32[]{:S(2)}, u32[]{:S(2)}) collective-permute-start(f32[8,256]{1,0:T(8,128)S(1)} %copy-done.6), channel_id=1, source_target_pairs={{0,4},{4,0},{1,5},{5,1},{2,6},{6,2},{3,7},{7,3},{8,12},{12,8},{9,1... | collective-permute-start | bytes 24584 | tf_op jit(solution)/shard_map/ppermute | solution.py:298
  36.5 1.5 %all-to-all-done.1.tiles_ref = f32[8,40,128]{2,1,0:T(8,128)S(1)} async-done(((f32[8,40,128]{2,1,0:T(8,128)}), f32[8,40,128]{2,1,0:T(8,128)S(1)}, u32[]{:S(2)}, u32[]{:S(2)}) %all-to-all-start.1) | async-done | bytes 163872 | tf_op jit(solution)/shard_map/all_to_all | solution.py:280
  38.0 3.5 %collective-permute-start = (f32[16,128]{1,0:T(8,128)S(1)}, f32[16,128]{1,0:T(8,128)S(1)}, u32[]{:S(2)}, u32[]{:S(2)}) collective-permute-start(f32[16,128]{1,0:T(8,128)S(1)} %shard_map.97), channel_id=1, source_target_pairs={{0,32},{32,0},{1,33},{33,1},{2,34},{34,2},{3,35},{35,3},{4,36},{36... | collective-permute-start | bytes 24584 | tf_op jit(solution)/shard_map/ppermute | solution.py:276
  42.2 0.0 collective-permute-done.1.twin_ref
  42.2 0.2 collective-permute-done.other_ref
  42.4 11.3 %all_to_all.31 = f32[16,40,128]{2,1,0:T(8,128)S(1)} all-to-all(f32[16,40,128]{2,1,0:T(8,128)S(1)} %get-tuple-element.17), channel_id=1, replica_groups=mesh['section_0'=4,'section_1'=2,'dom_0'=4,'dom_1'=2,'dom_2'=4] {'dom_0'..., dimensions={0} | all-to-all | bytes 655360 | tf_op jit(solution)/shard_map/all_to_all | solution.py:280
  53.7 0.0 copy-done.3
  53.7 0.0 copy-done.5
  53.7 0.0 copy-start.1
  53.7 2.8 %copy-done.1 = f32[8,2,6,128,128]{4,3,2,1,0:T(8,128)S(1)} copy-done((f32[8,2,6,128,128]{4,3,2,1,0:T(8,128)S(1)}, f32[8,2,6,128,128]{4,3,2,1,0:T(8,128)}, u32[]{:S(2)}) %copy-start.1) | copy-done | bytes 6291480
  56.4 0.0 copy-start.2
  56.4 1.7 %shard_map.99 = (f32[8,256]{1,0:T(8,128)S(1)}, f32[640,128]{1,0:T(8,128)S(1)}) custom-call(s32[96]{0:T(128)S(1)} %get-tuple-element.14.index_in, f32[1]{0:T(128)S(6)} %copy.10.weight_ref, f32[8,2,6,128,128]{4,3,2,1,0:T(8,128)S(1)} %copy-done.1, f32[640,128]{1,0:T(8,128)S(1)} %bitcast.7, f32[8,256]{1,0:T(8,128)S(1)} %copy-done.3, f32[8,256]{1,0:T(8,128)S(1)} %copy-done.5, ...), custom_call_target="tpu_custom_call" | custom-call | tf_op jit(solution)/shard_map/pallas_call | solution.py:330
  58.2 10.9 %all_to_all.32.pieces_ref = f32[16,40,128]{2,1,0:T(8,128)S(1)} all-to-all(f32[16,40,128]{2,1,0:T(8,128)S(1)} %bitcast.8), channel_id=1, replica_groups=mesh['section_0'=4,'section_1'=2,'dom_0'=4,'dom_1'=2,'dom_2'=4] {'dom_0'..., dimensions={0} | all-to-all | bytes 655360 | tf_op jit(solution)/shard_map/all_to_all | solution.py:280
  69.1 9.8 %all_to_all.33.tiles_ref = f32[8,40,128]{2,1,0:T(8,128)S(1)} all-to-all(f32[8,40,128]{2,1,0:T(8,128)S(1)} %shard_map.100), channel_id=1, replica_groups=mesh['section_0'=4,'section_1'=2,'dom_0'=4,'dom_1'=2,'dom_2'=4] {'sectio..., dimensions={0} | all-to-all | bytes 327680 | tf_op jit(solution)/shard_map/all_to_all | solution.py:280
  78.9 5.8 %collective-permute-start.2 = (f32[16,128]{1,0:T(8,128)S(1)}, f32[16,128]{1,0:T(8,128)S(1)}, u32[]{:S(2)}, u32[]{:S(2)}) collective-permute-start(f32[16,128]{1,0:T(8,128)S(1)} %shard_map.101), channel_id=1, source_target_pairs={{0,32},{32,0},{1,33},{33,1},{2,34},{34,2},{3,35},{35,3},{4,36},{36... | collective-permute-start | bytes 24584 | tf_op jit(solution)/shard_map/ppermute | solution.py:276
  84.7 0.8 collective-permute-done.2.other_ref
  85.5 0.1 shard_map.102
  85.7 11.5 %all_to_all.34 = f32[16,40,128]{2,1,0:T(8,128)S(1)} all-to-all(f32[16,40,128]{2,1,0:T(8,128)S(1)} %get-tuple-element.22), channel_id=1, replica_groups=mesh['section_0'=4,'section_1'=2,'dom_0'=4,'dom_1'=2,'dom_2'=4] {'dom_0'..., dimensions={0} | all-to-all | bytes 655360 | tf_op jit(solution)/shard_map/all_to_all | solution.py:280
  97.2 0.0 copy-done.2
  97.2 1.7 %shard_map.103 = (f32[8,256]{1,0:T(8,128)}, f32[8,256]{1,0:T(8,128)}) custom-call(s32[96]{0:T(128)S(1)} %get-tuple-element.14.index_in, f32[8,2,6,128,128]{4,3,2,1,0:T(8,128)S(1)} %copy-done.2, f32[640,128]{1,0:T(8,128)S(1)} %bitcast.6, f32[8,128]{1,0:T(8,128)S(1)} %get-tuple-element.23.steps_ref, f32[8,256]{1,0:T(8,128)S(1)} %get-tuple-element.24.dual_ref, ...), custom_call_target="tpu_custom_call" | custom-call | tf_op jit(solution)/shard_map/pallas_call | solution.py:343
  (4 shorter events, 0.1 us)
Async XLA Ops:
  0.6 53.0 %copy-start.3 = (f32[8,256]{1,0:T(8,128)S(1)}, f32[8,256]{1,0:T(8,128)}, u32[]{:S(2)}) copy-start(f32[8,256]{1,0:T(8,128)} %dual_ref.1) | copy-start | bytes 24580
  0.6 21.6 %copy-start.6 = (f32[8,256]{1,0:T(8,128)S(1)}, f32[8,256]{1,0:T(8,128)}, u32[]{:S(2)}) copy-start(f32[8,256]{1,0:T(8,128)} %primal_ref.3) | copy-start | bytes 24580
  0.7 21.6 %copy-start.4 = (f32[8,256]{1,0:T(8,128)S(1)}, f32[8,256]{1,0:T(8,128)}, u32[]{:S(2)}) copy-start(f32[8,256]{1,0:T(8,128)} %cost_ref.3) | copy-start | bytes 24580
  0.7 53.0 %copy-start.5 = (f32[8,256]{1,0:T(8,128)S(1)}, f32[8,256]{1,0:T(8,128)}, u32[]{:S(2)}) copy-start(f32[8,256]{1,0:T(8,128)} %demand_ref.3) | copy-start | bytes 24580
  3.7 2.7 %copy-start = (f32[8,2,6,128,128]{4,3,2,1,0:T(8,128)}, f32[8,2,6,128,128]{4,3,2,1,0:T(8,128)S(1)}, u32[]{:S(2)}) copy-start(f32[8,2,6,128,128]{4,3,2,1,0:T(8,128)S(1)} %get-tuple-element.15.blocks_ref) | copy-start | bytes 18874372
  23.0 15.1 %all-to-all-start.1 = ((f32[8,40,128]{2,1,0:T(8,128)}), f32[8,40,128]{2,1,0:T(8,128)S(1)}, u32[]{:S(2)}, u32[]{:S(2)}) async-start(f32[8,40,128]{2,1,0:T(8,128)} %shard_map.96), calls=%async_computation.1 | async-start | bytes 327680 | tf_op jit(solution)/shard_map/all_to_all | solution.py:280
  31.1 11.0 %collective-permute-start.1 = (f32[8,256]{1,0:T(8,128)S(1)}, f32[8,256]{1,0:T(8,128)S(1)}, u32[]{:S(2)}, u32[]{:S(2)}) collective-permute-start(f32[8,256]{1,0:T(8,128)S(1)} %copy-done.6), channel_id=1, source_target_pairs={{0,4},{4,0},{1,5},{5,1},{2,6},{6,2},{3,7},{7,3},{8,12},{12,8},{9,1... | collective-permute-start | bytes 24584 | tf_op jit(solution)/shard_map/ppermute | solution.py:298
  38.0 4.3 %collective-permute-start = (f32[16,128]{1,0:T(8,128)S(1)}, f32[16,128]{1,0:T(8,128)S(1)}, u32[]{:S(2)}, u32[]{:S(2)}) collective-permute-start(f32[16,128]{1,0:T(8,128)S(1)} %shard_map.97), channel_id=1, source_target_pairs={{0,32},{32,0},{1,33},{33,1},{2,34},{34,2},{3,35},{35,3},{4,36},{36... | collective-permute-start | bytes 24584 | tf_op jit(solution)/shard_map/ppermute | solution.py:276
  53.7 2.8 %copy-start.1 = (f32[8,2,6,128,128]{4,3,2,1,0:T(8,128)S(1)}, f32[8,2,6,128,128]{4,3,2,1,0:T(8,128)}, u32[]{:S(2)}) copy-start(f32[8,2,6,128,128]{4,3,2,1,0:T(8,128)} %copy-done) | copy-start | bytes 18874372
  56.4 40.7 %copy-start.2 = (f32[8,2,6,128,128]{4,3,2,1,0:T(8,128)S(1)}, f32[8,2,6,128,128]{4,3,2,1,0:T(8,128)}, u32[]{:S(2)}) copy-start(f32[8,2,6,128,128]{4,3,2,1,0:T(8,128)} %copy-done) | copy-start | bytes 18874372
  78.9 6.6 %collective-permute-start.2 = (f32[16,128]{1,0:T(8,128)S(1)}, f32[16,128]{1,0:T(8,128)S(1)}, u32[]{:S(2)}, u32[]{:S(2)}) collective-permute-start(f32[16,128]{1,0:T(8,128)S(1)} %shard_map.101), channel_id=1, source_target_pairs={{0,32},{32,0},{1,33},{33,1},{2,34},{34,2},{3,35},{35,3},{4,36},{36... | collective-permute-start | bytes 24584 | tf_op jit(solution)/shard_map/ppermute | solution.py:276

commit v5 on v4

--- a/solution.py
+++ b/solution.py
@@ -8,10 +8,10 @@
 from jax.sharding import Mesh
 from jax.sharding import PartitionSpec as P
 
-AXES = ("section_0", "section_1", "dom_0", "dom_1", "dom_2")
+AXES = ("section_0", "section_1", "dom_00", "dom_01", "dom_1", "dom_20", "dom_21")
 SECTION = ("section_0", "section_1")
-DOM = ("dom_0", "dom_1", "dom_2")
-PLANE = ("dom_0", "dom_2")
+DOM = ("dom_00", "dom_01", "dom_1", "dom_20", "dom_21")
+PLANE = ("dom_21", "dom_20", "dom_00", "dom_01")
 TWIN = "dom_1"
 LINE = ("section_0", "dom_1")
 CORE = "section_1"
@@ -91,7 +91,7 @@
         for k in range(6):
             c = column_ref[k, r, t]
             before = lax.axis_index(SECTION) * PERIODS_HERE + t - period_ref[k, r, t]
-            peer = (c >> 4) * 4 + ((c >> 1) & 3)
+            peer = ((c >> 1) & 1) * 8 + ((c >> 2) & 1) * 4 + ((c >> 5) & 1) * 2 + ((c >> 4) & 1) * 1
             inside = ((c >> 3) & 1) * 2 + (c & 1)
             row = inside * 8 + t - before
             if t == 0:
@@ -149,8 +149,8 @@
 
 def sum_first(pieces_ref, cost_ref, primal_ref, tiles_ref, tile):
     tile_of(tile, pieces_ref, cost_ref)
-    tile[36:37, :] = primal_ref[7:8, :128]
-    tile[37:38, :] = primal_ref[7:8, 128:]
+    tile[40:48, :] = primal_ref[:, :128]
+    tile[48:56, :] = primal_ref[:, 128:]
     to_all(tiles_ref, tile[...], LINE_PEERS)
 
 
@@ -168,8 +168,10 @@
     pack_ref[...] = jnp.zeros_like(pack_ref)
     pack_ref[0:4, :] = tiles_ref[above, HALO] + tiles_ref[above + 1, HALO]
     pack_ref[4:8, :] = tiles_ref[below, last] + tiles_ref[below + 1, last]
-    pack_ref[8:10, :] = tiles_ref[below, 36:38]
-    pack_ref[10:12, :] = tiles_ref[below + 1, 36:38]
+    if tiles_ref.shape[1] > PIECE:
+        late = pl.ds(47, 2, stride=8)
+        pack_ref[8:10, :] = tiles_ref[below, late]
+        pack_ref[10:12, :] = tiles_ref[below + 1, late]
     moves = tiles_ref[0, 36:40]
     for d in range(1, LINE_PEERS):
         moves = moves + tiles_ref[d, 36:40]
@@ -190,16 +192,12 @@
 
 
 def primal_step(
-    weight_ref, tiles_ref, other_ref, primal_ref, twin_ref, copies_ref, primal_one_ref, before_one_ref, move_ref,
-    descent,
+    weight_ref, tiles_ref, other_ref, copies_ref, primal_one_ref, before_one_ref, move_ref, descent
 ):
     tau = step_scale / jnp.full((1, 128), weight_ref[0], f32)
     along, along_before = descents(tiles_ref, other_ref, descent)
-    first = lax.axis_index(TWIN) == 0
-    own, twin = (
-        jnp.concatenate([ref[:, :128], ref[:, 128:]], 0) for ref in (primal_ref, twin_ref)
-    )
-    start = jnp.concatenate([jnp.where(first, own, twin), jnp.where(first, twin, own)], 0)
+    here = 2 * lax.axis_index("section_0")
+    start = jnp.concatenate([tiles_ref[here, 40:56], tiles_ref[here + 1, 40:56]], 0)
     start_before = other_ref[8:12]
     primal_one = jnp.maximum(0.0, start + tau * along)
     before_one = jnp.maximum(0.0, start_before + tau * along_before)
@@ -293,9 +291,6 @@
     local = shaped(8, 256)
     pack = shaped(16, 128)
     rows = pltpu.VMEM((CHUNK, 128), f32)
-    tile = shaped(LINE_PEERS, PIECE, 128)
-    rows_of_tile = [pltpu.VMEM((PIECE, 128), f32)]
-    primal_twin = lax.ppermute(primal_start, TWIN, [(0, 1), (1, 0)])
 
     places = [pltpu.SMEM((96,), jnp.int32), pltpu.SemaphoreType.DMA(())]
     index, partial, kept = call(
@@ -317,15 +312,17 @@
     )
     kept = pltpu.with_memory_space_constraint(kept, pltpu.VMEM)
     arrived = exchange(partial.reshape(pieces), PLANE)
-    tiles = call(sum_first, tile, [VMEM] * 3, rows_of_tile)(arrived, cost_vector, primal_start)
+    tiles = call(
+        sum_first, shaped(LINE_PEERS, 56, 128), [VMEM] * 3, [pltpu.VMEM((56, 128), f32)]
+    )(arrived, cost_vector, primal_start)
     tiles = exchange(tiles, LINE)
     other = to_other_core(call(for_other_core, pack, [VMEM])(tiles))
     send, primal_one, before_one, move_primal = call(
         primal_step,
         [shaped(*pieces), chunk, shaped(4, 128), shaped(1, 128)],
-        [SMEM] + [VMEM] * 4,
+        [SMEM, VMEM, VMEM],
         [rows],
-    )(primal_weight, tiles, other, primal_start, primal_twin)
+    )(primal_weight, tiles, other)
     field = exchange(send, PLANE).reshape(PEERS * PIECE, 128)
     dual_one, partial = call(
         dual_step, [local, partials], [VMEM, SMEM] + [VMEM] * 5, places
@@ -333,7 +330,9 @@
         index, primal_weight, kept, field, dual_start, demand, move_primal
     )
     arrived = exchange(partial.reshape(pieces), PLANE)
-    tiles = call(sum_second, tile, [VMEM] * 2, rows_of_tile)(arrived, cost_vector)
+    tiles = call(sum_second, shaped(LINE_PEERS, PIECE, 128), [VMEM] * 2, [pltpu.VMEM((PIECE, 128), f32)])(
+        arrived, cost_vector
+    )
     tiles = exchange(tiles, LINE)
     other = to_other_core(call(for_other_core, pack, [VMEM])(tiles))
     send, primal, steps = call(
@@ -347,7 +346,7 @@
 
 
 def solution(mesh):
-    finer = Mesh(mesh.devices.reshape(4, 2, 4, 2, 4), AXES)
+    finer = Mesh(mesh.devices.reshape(4, 2, 2, 2, 2, 2, 2), AXES)
     return jax.shard_map(
         on_device,
         mesh=finer,

time: 99.2 us -> 91.3 us (0.920)
  starting transfers between devices: 22.8 us -> 8.59 us
  blocking collectives: 59.3 us -> 72.9 us
  local copies, waits for them, and re-layouts: 5.45 us -> 0.02 us
  waiting for transfers between devices: 2.51 us -> 1.01 us
    all_to_all x5 -> x6, blocking collectives: 59.3 us -> 72.9 us  [exchange(): return lax.all_to_all(pieces, axis, split_axis=0, concat_axis=0, tiled=True)]
    all_to_all x1 -> x0, starting transfers between devices: 8.18 us -> none  [exchange(): return lax.all_to_all(pieces, axis, split_axis=0, concat_axis=0, tiled=True)]
    unnamed x14 -> x8, local copies, waits for them, and re-layouts: 5.45 us -> 0.02 us
    ppermute x1 -> x0, starting transfers between devices: 5.37 us -> none  [on_device(): primal_twin = lax.ppermute(primal_start, TWIN, [(0, 1), (1, 0)])]
    all_to_all x1 -> x0, waiting for transfers between devices: 1.51 us -> none  [exchange(): return lax.all_to_all(pieces, axis, split_axis=0, concat_axis=0, tiled=True)]
  transfers between devices with their start and end apart: 4 -> 2, of which waited for: 3 -> 2; matrix products, arithmetic and copies ran while one was open for 0% -> 0% of each run, Pallas kernels for 0% -> 0%
where the time goes in v5:
time: 91.3 us; the launch traced here: 90.6 us
  blocking collectives  72.9 us (80%)
  starting transfers between devices  8.59 us (9%)
  Pallas kernels  6.75 us (7%)
  between operations  1.36 us (1%)
  waiting for transfers between devices  1.01 us (1%)
    all_to_all x6, blocking collectives, exchange(): return lax.all_to_all(pieces, axis, split_axis=0, concat_axis=0, tiled=True)  72.9 us
    ppermute x2, starting transfers between devices, to_other_core(): return lax.ppermute(x, CORE, [(0, 1), (1, 0)])  8.59 us
    pallas_call x1, Pallas kernels, on_device(): call(adjoint_start, [jax.ShapeDtypeStruct((96,), jnp.int32), partials, sh...  3.09 us
  transfers between devices with their start and end apart: 2, of which 2 were waited for; matrix products, arithmetic and copies ran while one was open for 0% of the time, Pallas kernels for 0%

profile of v5, /device:TPU:1, one launch (start us, length us, event | category | flops | bytes accessed | tf_op | source)
XLA Modules:
  0.0 90.6 jit_solution(2748011308523789969)
XLA Ops:
  0.6 0.0 copy-start
  0.6 0.0 copy-start.1
  0.7 0.0 copy-start.3
  0.7 0.0 copy-start.2
  0.7 3.1 %shard_map.95 = (s32[96]{0:T(128)S(1)}, f32[640,128]{1,0:T(8,128)S(1)}, f32[8,2,6,128,128]{4,3,2,1,0:T(8,128)S(1)}) custom-call(s32[6,2,8]{2,1,0:T(2,128)} %bitcast.10, s32[6,2,8]{2,1,0:T(2,128)} %bitcast.11, f32[8,2,6,128,128]{4,3,2,1,0:T(8,128)} %blocks_in.1, f32[8,256]{1,0:T(8,128)} %dual_ref.1), custom_call_target="tpu_custom_call" | custom-call | tf_op jit(solution)/shard_map/pallas_call | solution.py:296
  3.8 15.3 %all_to_all.30.pieces_ref = f32[16,40,128]{2,1,0:T(8,128)S(1)} all-to-all(f32[16,40,128]{2,1,0:T(8,128)S(1)} %bitcast.9), channel_id=1, replica_groups=mesh['section_0'=4,'section_1'=2,'dom_00'=2,'dom_01'=2,'dom_1'=2,'dom_20..., dimensions={0} | all-to-all | bytes 655360 | tf_op jit(solution)/shard_map/all_to_all | solution.py:278
  19.1 0.0 copy-done.1
  19.1 0.0 copy-done.3
  19.1 15.0 %all_to_all.31.tiles_ref = f32[8,56,128]{2,1,0:T(8,128)S(1)} all-to-all(f32[8,56,128]{2,1,0:T(8,128)S(1)} %shard_map.96), channel_id=1, replica_groups=mesh['section_0'=4,'section_1'=2,'dom_00'=2,'dom_01'=2,'dom_1'=2,'dom_20..., dimensions={0} | all-to-all | bytes 458752 | tf_op jit(solution)/shard_map/all_to_all | solution.py:278
  34.1 4.0 %collective-permute-start = (f32[16,128]{1,0:T(8,128)S(1)}, f32[16,128]{1,0:T(8,128)S(1)}, u32[]{:S(2)}, u32[]{:S(2)}) collective-permute-start(f32[16,128]{1,0:T(8,128)S(1)} %shard_map.97), channel_id=1, source_target_pairs={{0,32},{32,0},{1,33},{33,1},{2,34},{34,2},{3,35},{35,3},{4,36},{36... | collective-permute-start | bytes 24584 | tf_op jit(solution)/shard_map/ppermute | solution.py:274
  38.7 0.2 collective-permute-done.other_ref
  39.0 11.1 %all_to_all.32 = f32[16,40,128]{2,1,0:T(8,128)S(1)} all-to-all(f32[16,40,128]{2,1,0:T(8,128)S(1)} %get-tuple-element.17), channel_id=1, replica_groups=mesh['section_0'=4,'section_1'=2,'dom_00'=2,'dom_01'=2,'dom_1'=2,'dom_20..., dimensions={0} | all-to-all | bytes 655360 | tf_op jit(solution)/shard_map/all_to_all | solution.py:278
  50.1 0.0 copy-done
  50.1 0.0 copy-done.2
  50.1 1.7 %shard_map.99 = (f32[8,256]{1,0:T(8,128)S(1)}, f32[640,128]{1,0:T(8,128)S(1)}) custom-call(s32[96]{0:T(128)S(1)} %get-tuple-element.14.index_in, f32[1]{0:T(128)S(6)} %copy.10.weight_ref, f32[8,2,6,128,128]{4,3,2,1,0:T(8,128)S(1)} %get-tuple-element.15.blocks_ref, f32[640,128]{1,0:T(8,128)S(1)} %bitcast.7, f32[8,256]{1,0:T(8,128)S(1)} %copy-done, ...), custom_call_target="tpu_custom_call" | custom-call | tf_op jit(solution)/shard_map/pallas_call | solution.py:327
  51.8 10.7 %all_to_all.33.pieces_ref = f32[16,40,128]{2,1,0:T(8,128)S(1)} all-to-all(f32[16,40,128]{2,1,0:T(8,128)S(1)} %bitcast.8), channel_id=1, replica_groups=mesh['section_0'=4,'section_1'=2,'dom_00'=2,'dom_01'=2,'dom_1'=2,'dom_20..., dimensions={0} | all-to-all | bytes 655360 | tf_op jit(solution)/shard_map/all_to_all | solution.py:278
  62.5 9.8 %all_to_all.34.tiles_ref = f32[8,40,128]{2,1,0:T(8,128)S(1)} all-to-all(f32[8,40,128]{2,1,0:T(8,128)S(1)} %shard_map.100), channel_id=1, replica_groups=mesh['section_0'=4,'section_1'=2,'dom_00'=2,'dom_01'=2,'dom_1'=2,'dom_20..., dimensions={0} | all-to-all | bytes 327680 | tf_op jit(solution)/shard_map/all_to_all | solution.py:278
  72.3 4.6 %collective-permute-start.1 = (f32[16,128]{1,0:T(8,128)S(1)}, f32[16,128]{1,0:T(8,128)S(1)}, u32[]{:S(2)}, u32[]{:S(2)}) collective-permute-start(f32[16,128]{1,0:T(8,128)S(1)} %shard_map.101), channel_id=1, source_target_pairs={{0,32},{32,0},{1,33},{33,1},{2,34},{34,2},{3,35},{35,3},{4,36},{36... | collective-permute-start | bytes 24584 | tf_op jit(solution)/shard_map/ppermute | solution.py:274
  76.9 0.8 collective-permute-done.1.other_ref
  77.8 0.1 shard_map.102
  77.9 11.0 %all_to_all.35 = f32[16,40,128]{2,1,0:T(8,128)S(1)} all-to-all(f32[16,40,128]{2,1,0:T(8,128)S(1)} %get-tuple-element.22), channel_id=1, replica_groups=mesh['section_0'=4,'section_1'=2,'dom_00'=2,'dom_01'=2,'dom_1'=2,'dom_20..., dimensions={0} | all-to-all | bytes 655360 | tf_op jit(solution)/shard_map/all_to_all | solution.py:278
  88.9 1.7 %shard_map.103 = (f32[8,256]{1,0:T(8,128)}, f32[8,256]{1,0:T(8,128)}) custom-call(s32[96]{0:T(128)S(1)} %get-tuple-element.14.index_in, f32[8,2,6,128,128]{4,3,2,1,0:T(8,128)S(1)} %get-tuple-element.15.blocks_ref, f32[640,128]{1,0:T(8,128)S(1)} %bitcast.6, f32[8,128]{1,0:T(8,128)S(1)} %get-tuple-element.23.steps_ref, ...), custom_call_target="tpu_custom_call" | custom-call | tf_op jit(solution)/shard_map/pallas_call | solution.py:342
  (5 shorter events, 0.1 us)
Async XLA Ops:
  0.6 49.5 %copy-start = (f32[8,256]{1,0:T(8,128)S(1)}, f32[8,256]{1,0:T(8,128)}, u32[]{:S(2)}) copy-start(f32[8,256]{1,0:T(8,128)} %dual_ref.1) | copy-start | bytes 24580
  0.6 18.4 %copy-start.1 = (f32[8,256]{1,0:T(8,128)S(1)}, f32[8,256]{1,0:T(8,128)}, u32[]{:S(2)}) copy-start(f32[8,256]{1,0:T(8,128)} %cost_ref.3) | copy-start | bytes 24580
  0.7 18.4 %copy-start.3 = (f32[8,256]{1,0:T(8,128)S(1)}, f32[8,256]{1,0:T(8,128)}, u32[]{:S(2)}) copy-start(f32[8,256]{1,0:T(8,128)} %primal_ref.1) | copy-start | bytes 24580
  0.7 49.4 %copy-start.2 = (f32[8,256]{1,0:T(8,128)S(1)}, f32[8,256]{1,0:T(8,128)}, u32[]{:S(2)}) copy-start(f32[8,256]{1,0:T(8,128)} %demand_ref.3) | copy-start | bytes 24580
  34.1 4.8 %collective-permute-start = (f32[16,128]{1,0:T(8,128)S(1)}, f32[16,128]{1,0:T(8,128)S(1)}, u32[]{:S(2)}, u32[]{:S(2)}) collective-permute-start(f32[16,128]{1,0:T(8,128)S(1)} %shard_map.97), channel_id=1, source_target_pairs={{0,32},{32,0},{1,33},{33,1},{2,34},{34,2},{3,35},{35,3},{4,36},{36... | collective-permute-start | bytes 24584 | tf_op jit(solution)/shard_map/ppermute | solution.py:274
  72.3 5.5 %collective-permute-start.1 = (f32[16,128]{1,0:T(8,128)S(1)}, f32[16,128]{1,0:T(8,128)S(1)}, u32[]{:S(2)}, u32[]{:S(2)}) collective-permute-start(f32[16,128]{1,0:T(8,128)S(1)} %shard_map.101), channel_id=1, source_target_pairs={{0,32},{32,0},{1,33},{33,1},{2,34},{34,2},{3,35},{35,3},{4,36},{36... | collective-permute-start | bytes 24584 | tf_op jit(solution)/shard_map/ppermute | solution.py:274

commit v6 on v5

--- a/solution.py
+++ b/solution.py
@@ -164,14 +164,15 @@
     core = lax.axis_index(CORE)
     above = 2 * jnp.minimum(chip + 1 - core, 3)
     below = 2 * jnp.maximum(chip - core, 0)
-    last = pl.ds(7, 4, stride=8)
     pack_ref[...] = jnp.zeros_like(pack_ref)
     pack_ref[0:4, :] = tiles_ref[above, HALO] + tiles_ref[above + 1, HALO]
-    pack_ref[4:8, :] = tiles_ref[below, last] + tiles_ref[below + 1, last]
+    for i in range(4):
+        last = slice(8 * i + 7, 8 * i + 8)
+        pack_ref[4 + i : 5 + i, :] = tiles_ref[below, last] + tiles_ref[below + 1, last]
     if tiles_ref.shape[1] > PIECE:
-        late = pl.ds(47, 2, stride=8)
-        pack_ref[8:10, :] = tiles_ref[below, late]
-        pack_ref[10:12, :] = tiles_ref[below + 1, late]
+        for i in range(4):
+            late = 47 + 8 * (i % 2)
+            pack_ref[8 + i : 9 + i, :] = tiles_ref[below + i // 2, late : late + 1]
     moves = tiles_ref[0, 36:40]
     for d in range(1, LINE_PEERS):
         moves = moves + tiles_ref[d, 36:40]
@@ -182,7 +183,9 @@
     section = lax.axis_index(SECTION)
     here = 2 * lax.axis_index("section_0")
     descent[...] = tiles_ref[here, 0:CHUNK] + tiles_ref[here + 1, 0:CHUNK]
-    descent[pl.ds(7, 4, stride=8), :] += jnp.where(section < 7, other_ref[0:4], 0.0)
+    for i in range(4):
+        carried = jnp.where(section < 7, other_ref[i : i + 1], 0.0)
+        descent[8 * i + 7 : 8 * i + 8, :] += carried
     before = other_ref[4:8] + tiles_ref[here, HALO] + tiles_ref[here + 1, HALO]
     return descent[...], before
 

time: 91.3 us -> 91.3 us (level)
  no operation moved by 1% of the time
where the time goes in v6:
time: 91.3 us; the launch traced here: 90.6 us
  blocking collectives  72.9 us (80%)
  starting transfers between devices  8.6 us (9%)
  Pallas kernels  6.77 us (7%)
  between operations  1.36 us (1%)
  waiting for transfers between devices  1.01 us (1%)
    all_to_all x6, blocking collectives, exchange(): return lax.all_to_all(pieces, axis, split_axis=0, concat_axis=0, tiled=True)  72.9 us
    ppermute x2, starting transfers between devices, to_other_core(): return lax.ppermute(x, CORE, [(0, 1), (1, 0)])  8.6 us
    pallas_call x1, Pallas kernels, on_device(): call(adjoint_start, [jax.ShapeDtypeStruct((96,), jnp.int32), partials, sh...  3.09 us
  transfers between devices with their start and end apart: 2, of which 2 were waited for; matrix products, arithmetic and copies ran while one was open for 0% of the time, Pallas kernels for 0%

profile of v6, /device:TPU:1, one launch (start us, length us, event | category | flops | bytes accessed | tf_op | source)
XLA Modules:
  0.0 90.6 jit_solution(4528471997774515162)
XLA Ops:
  0.6 0.0 copy-start
  0.6 0.0 copy-start.1
  0.7 0.0 copy-start.3
  0.7 0.0 copy-start.2
  0.7 3.1 %shard_map.95 = (s32[96]{0:T(128)S(1)}, f32[640,128]{1,0:T(8,128)S(1)}, f32[8,2,6,128,128]{4,3,2,1,0:T(8,128)S(1)}) custom-call(s32[6,2,8]{2,1,0:T(2,128)} %bitcast.10, s32[6,2,8]{2,1,0:T(2,128)} %bitcast.11, f32[8,2,6,128,128]{4,3,2,1,0:T(8,128)} %blocks_in.1, f32[8,256]{1,0:T(8,128)} %dual_ref.1), custom_call_target="tpu_custom_call" | custom-call | tf_op jit(solution)/shard_map/pallas_call | solution.py:299
  3.8 15.3 %all_to_all.30.pieces_ref = f32[16,40,128]{2,1,0:T(8,128)S(1)} all-to-all(f32[16,40,128]{2,1,0:T(8,128)S(1)} %bitcast.9), channel_id=1, replica_groups=mesh['section_0'=4,'section_1'=2,'dom_00'=2,'dom_01'=2,'dom_1'=2,'dom_20..., dimensions={0} | all-to-all | bytes 655360 | tf_op jit(solution)/shard_map/all_to_all | solution.py:281
  19.1 0.0 copy-done.1
  19.1 0.0 copy-done.3
  19.2 15.0 %all_to_all.31.tiles_ref = f32[8,56,128]{2,1,0:T(8,128)S(1)} all-to-all(f32[8,56,128]{2,1,0:T(8,128)S(1)} %shard_map.96), channel_id=1, replica_groups=mesh['section_0'=4,'section_1'=2,'dom_00'=2,'dom_01'=2,'dom_1'=2,'dom_20..., dimensions={0} | all-to-all | bytes 458752 | tf_op jit(solution)/shard_map/all_to_all | solution.py:281
  34.1 4.0 %collective-permute-start = (f32[16,128]{1,0:T(8,128)S(1)}, f32[16,128]{1,0:T(8,128)S(1)}, u32[]{:S(2)}, u32[]{:S(2)}) collective-permute-start(f32[16,128]{1,0:T(8,128)S(1)} %shard_map.97), channel_id=1, source_target_pairs={{0,32},{32,0},{1,33},{33,1},{2,34},{34,2},{3,35},{35,3},{4,36},{36... | collective-permute-start | bytes 24584 | tf_op jit(solution)/shard_map/ppermute | solution.py:277
  38.7 0.2 collective-permute-done.other_ref
  39.0 11.1 %all_to_all.32 = f32[16,40,128]{2,1,0:T(8,128)S(1)} all-to-all(f32[16,40,128]{2,1,0:T(8,128)S(1)} %get-tuple-element.17), channel_id=1, replica_groups=mesh['section_0'=4,'section_1'=2,'dom_00'=2,'dom_01'=2,'dom_1'=2,'dom_20..., dimensions={0} | all-to-all | bytes 655360 | tf_op jit(solution)/shard_map/all_to_all | solution.py:281
  50.1 0.0 copy-done
  50.1 0.0 copy-done.2
  50.1 1.7 %shard_map.99 = (f32[8,256]{1,0:T(8,128)S(1)}, f32[640,128]{1,0:T(8,128)S(1)}) custom-call(s32[96]{0:T(128)S(1)} %get-tuple-element.14.index_in, f32[1]{0:T(128)S(6)} %copy.10.weight_ref, f32[8,2,6,128,128]{4,3,2,1,0:T(8,128)S(1)} %get-tuple-element.15.blocks_ref, f32[640,128]{1,0:T(8,128)S(1)} %bitcast.7, f32[8,256]{1,0:T(8,128)S(1)} %copy-done, ...), custom_call_target="tpu_custom_call" | custom-call | tf_op jit(solution)/shard_map/pallas_call | solution.py:330
  51.8 10.7 %all_to_all.33.pieces_ref = f32[16,40,128]{2,1,0:T(8,128)S(1)} all-to-all(f32[16,40,128]{2,1,0:T(8,128)S(1)} %bitcast.8), channel_id=1, replica_groups=mesh['section_0'=4,'section_1'=2,'dom_00'=2,'dom_01'=2,'dom_1'=2,'dom_20..., dimensions={0} | all-to-all | bytes 655360 | tf_op jit(solution)/shard_map/all_to_all | solution.py:281
  62.5 9.8 %all_to_all.34.tiles_ref = f32[8,40,128]{2,1,0:T(8,128)S(1)} all-to-all(f32[8,40,128]{2,1,0:T(8,128)S(1)} %shard_map.100), channel_id=1, replica_groups=mesh['section_0'=4,'section_1'=2,'dom_00'=2,'dom_01'=2,'dom_1'=2,'dom_20..., dimensions={0} | all-to-all | bytes 327680 | tf_op jit(solution)/shard_map/all_to_all | solution.py:281
  72.3 4.6 %collective-permute-start.1 = (f32[16,128]{1,0:T(8,128)S(1)}, f32[16,128]{1,0:T(8,128)S(1)}, u32[]{:S(2)}, u32[]{:S(2)}) collective-permute-start(f32[16,128]{1,0:T(8,128)S(1)} %shard_map.101), channel_id=1, source_target_pairs={{0,32},{32,0},{1,33},{33,1},{2,34},{34,2},{3,35},{35,3},{4,36},{36... | collective-permute-start | bytes 24584 | tf_op jit(solution)/shard_map/ppermute | solution.py:277
  76.9 0.8 collective-permute-done.1.other_ref
  77.8 0.1 shard_map.102
  77.9 11.0 %all_to_all.35 = f32[16,40,128]{2,1,0:T(8,128)S(1)} all-to-all(f32[16,40,128]{2,1,0:T(8,128)S(1)} %get-tuple-element.22), channel_id=1, replica_groups=mesh['section_0'=4,'section_1'=2,'dom_00'=2,'dom_01'=2,'dom_1'=2,'dom_20..., dimensions={0} | all-to-all | bytes 655360 | tf_op jit(solution)/shard_map/all_to_all | solution.py:281
  88.9 1.7 %shard_map.103 = (f32[8,256]{1,0:T(8,128)}, f32[8,256]{1,0:T(8,128)}) custom-call(s32[96]{0:T(128)S(1)} %get-tuple-element.14.index_in, f32[8,2,6,128,128]{4,3,2,1,0:T(8,128)S(1)} %get-tuple-element.15.blocks_ref, f32[640,128]{1,0:T(8,128)S(1)} %bitcast.6, f32[8,128]{1,0:T(8,128)S(1)} %get-tuple-element.23.steps_ref, ...), custom_call_target="tpu_custom_call" | custom-call | tf_op jit(solution)/shard_map/pallas_call | solution.py:345
  (5 shorter events, 0.1 us)
Async XLA Ops:
  0.6 49.5 %copy-start = (f32[8,256]{1,0:T(8,128)S(1)}, f32[8,256]{1,0:T(8,128)}, u32[]{:S(2)}) copy-start(f32[8,256]{1,0:T(8,128)} %dual_ref.1) | copy-start | bytes 24580
  0.6 18.5 %copy-start.1 = (f32[8,256]{1,0:T(8,128)S(1)}, f32[8,256]{1,0:T(8,128)}, u32[]{:S(2)}) copy-start(f32[8,256]{1,0:T(8,128)} %cost_ref.3) | copy-start | bytes 24580
  0.7 18.5 %copy-start.3 = (f32[8,256]{1,0:T(8,128)S(1)}, f32[8,256]{1,0:T(8,128)}, u32[]{:S(2)}) copy-start(f32[8,256]{1,0:T(8,128)} %primal_ref.1) | copy-start | bytes 24580
  0.7 49.4 %copy-start.2 = (f32[8,256]{1,0:T(8,128)S(1)}, f32[8,256]{1,0:T(8,128)}, u32[]{:S(2)}) copy-start(f32[8,256]{1,0:T(8,128)} %demand_ref.3) | copy-start | bytes 24580
  34.1 4.8 %collective-permute-start = (f32[16,128]{1,0:T(8,128)S(1)}, f32[16,128]{1,0:T(8,128)S(1)}, u32[]{:S(2)}, u32[]{:S(2)}) collective-permute-start(f32[16,128]{1,0:T(8,128)S(1)} %shard_map.97), channel_id=1, source_target_pairs={{0,32},{32,0},{1,33},{33,1},{2,34},{34,2},{3,35},{35,3},{4,36},{36... | collective-permute-start | bytes 24584 | tf_op jit(solution)/shard_map/ppermute | solution.py:277
  72.3 5.5 %collective-permute-start.1 = (f32[16,128]{1,0:T(8,128)S(1)}, f32[16,128]{1,0:T(8,128)S(1)}, u32[]{:S(2)}, u32[]{:S(2)}) collective-permute-start(f32[16,128]{1,0:T(8,128)S(1)} %shard_map.101), channel_id=1, source_target_pairs={{0,32},{32,0},{1,33},{33,1},{2,34},{34,2},{3,35},{35,3},{4,36},{36... | collective-permute-start | bytes 24584 | tf_op jit(solution)/shard_map/ppermute | solution.py:277

commit v7 on v6

--- a/solution.py
+++ b/solution.py
@@ -8,12 +8,13 @@
 from jax.sharding import Mesh
 from jax.sharding import PartitionSpec as P
 
-AXES = ("section_0", "section_1", "dom_00", "dom_01", "dom_1", "dom_20", "dom_21")
-SECTION = ("section_0", "section_1")
+AXES = ("section_00", "section_01", "section_1", "dom_00", "dom_01", "dom_1", "dom_20", "dom_21")
+SECTION = ("section_00", "section_01", "section_1")
 DOM = ("dom_00", "dom_01", "dom_1", "dom_20", "dom_21")
 PLANE = ("dom_21", "dom_20", "dom_00", "dom_01")
 TWIN = "dom_1"
-LINE = ("section_0", "dom_1")
+LINE = ("section_01", "section_00", "dom_1")
+CHIP = ("section_00", "section_01")
 CORE = "section_1"
 
 step_scale = 0.4
@@ -159,11 +160,15 @@
     to_all(tiles_ref, tile[...], LINE_PEERS)
 
 
+def tile_place(chip):
+    return (chip & 1) * 4 + (chip >> 1) * 2
+
+
 def for_other_core(tiles_ref, pack_ref):
-    chip = lax.axis_index("section_0")
+    chip = lax.axis_index(CHIP)
     core = lax.axis_index(CORE)
-    above = 2 * jnp.minimum(chip + 1 - core, 3)
-    below = 2 * jnp.maximum(chip - core, 0)
+    above = tile_place(jnp.minimum(chip + 1 - core, 3))
+    below = tile_place(jnp.maximum(chip - core, 0))
     pack_ref[...] = jnp.zeros_like(pack_ref)
     pack_ref[0:4, :] = tiles_ref[above, HALO] + tiles_ref[above + 1, HALO]
     for i in range(4):
@@ -181,7 +186,7 @@
 
 def descents(tiles_ref, other_ref, descent):
     section = lax.axis_index(SECTION)
-    here = 2 * lax.axis_index("section_0")
+    here = tile_place(lax.axis_index(CHIP))
     descent[...] = tiles_ref[here, 0:CHUNK] + tiles_ref[here + 1, 0:CHUNK]
     for i in range(4):
         carried = jnp.where(section < 7, other_ref[i : i + 1], 0.0)
@@ -199,7 +204,7 @@
 ):
     tau = step_scale / jnp.full((1, 128), weight_ref[0], f32)
     along, along_before = descents(tiles_ref, other_ref, descent)
-    here = 2 * lax.axis_index("section_0")
+    here = tile_place(lax.axis_index(CHIP))
     start = jnp.concatenate([tiles_ref[here, 40:56], tiles_ref[here + 1, 40:56]], 0)
     start_before = other_ref[8:12]
     primal_one = jnp.maximum(0.0, start + tau * along)
@@ -349,7 +354,7 @@
 
 
 def solution(mesh):
-    finer = Mesh(mesh.devices.reshape(4, 2, 2, 2, 2, 2, 2), AXES)
+    finer = Mesh(mesh.devices.reshape(2, 2, 2, 2, 2, 2, 2, 2), AXES)
     return jax.shard_map(
         on_device,
         mesh=finer,

time: 91.3 us -> 91 us (level)
  no operation moved by 1% of the time
where the time goes in v7:
time: 91 us; the launch traced here: 90.6 us
  blocking collectives  73 us (80%)
  starting transfers between devices  8.43 us (9%)
  Pallas kernels  6.77 us (7%)
  between operations  1.36 us (1%)
  waiting for transfers between devices  1.01 us (1%)
    all_to_all x6, blocking collectives, exchange(): return lax.all_to_all(pieces, axis, split_axis=0, concat_axis=0, tiled=True)  73 us
    ppermute x2, starting transfers between devices, to_other_core(): return lax.ppermute(x, CORE, [(0, 1), (1, 0)])  8.43 us
    pallas_call x1, Pallas kernels, on_device(): call(adjoint_start, [jax.ShapeDtypeStruct((96,), jnp.int32), partials, sh...  3.1 us
  transfers between devices with their start and end apart: 2, of which 2 were waited for; matrix products, arithmetic and copies ran while one was open for 0% of the time, Pallas kernels for 0%

profile of v7, /device:TPU:1, one launch (start us, length us, event | category | flops | bytes accessed | tf_op | source)
XLA Modules:
  0.0 90.6 jit_solution(12415614317069902832)
XLA Ops:
  0.6 0.0 copy-start
  0.6 0.0 copy-start.1
  0.7 0.0 copy-start.3
  0.7 0.0 copy-start.2
  0.7 3.1 %shard_map.95 = (s32[96]{0:T(128)S(1)}, f32[640,128]{1,0:T(8,128)S(1)}, f32[8,2,6,128,128]{4,3,2,1,0:T(8,128)S(1)}) custom-call(s32[6,2,8]{2,1,0:T(2,128)} %bitcast.10, s32[6,2,8]{2,1,0:T(2,128)} %bitcast.11, f32[8,2,6,128,128]{4,3,2,1,0:T(8,128)} %blocks_in.1, f32[8,256]{1,0:T(8,128)} %dual_ref.1), custom_call_target="tpu_custom_call" | custom-call | tf_op jit(solution)/shard_map/pallas_call | solution.py:304
  3.8 15.3 %all_to_all.30.pieces_ref = f32[16,40,128]{2,1,0:T(8,128)S(1)} all-to-all(f32[16,40,128]{2,1,0:T(8,128)S(1)} %bitcast.9), channel_id=1, replica_groups=mesh['section_00'=2,'section_01'=2,'section_1'=2,'dom_00'=2,'dom_01'=2,'..., dimensions={0} | all-to-all | bytes 655360 | tf_op jit(solution)/shard_map/all_to_all | solution.py:286
  19.1 0.0 copy-done.1
  19.1 0.0 copy-done.3
  19.1 15.0 %all_to_all.31.tiles_ref = f32[8,56,128]{2,1,0:T(8,128)S(1)} all-to-all(f32[8,56,128]{2,1,0:T(8,128)S(1)} %shard_map.96), channel_id=1, replica_groups=mesh['section_00'=2,'section_01'=2,'section_1'=2,'dom_00'=2,'dom_01'=2,'..., dimensions={0} | all-to-all | bytes 458752 | tf_op jit(solution)/shard_map/all_to_all | solution.py:286
  34.1 3.8 %collective-permute-start = (f32[16,128]{1,0:T(8,128)S(1)}, f32[16,128]{1,0:T(8,128)S(1)}, u32[]{:S(2)}, u32[]{:S(2)}) collective-permute-start(f32[16,128]{1,0:T(8,128)S(1)} %shard_map.97), channel_id=1, source_target_pairs={{0,32},{32,0},{1,33},{33,1},{2,34},{34,2},{3,35},{35,3},{4,36},{36... | collective-permute-start | bytes 24584 | tf_op jit(solution)/shard_map/ppermute | solution.py:282
  38.5 0.2 collective-permute-done.other_ref
  38.8 11.0 %all_to_all.32 = f32[16,40,128]{2,1,0:T(8,128)S(1)} all-to-all(f32[16,40,128]{2,1,0:T(8,128)S(1)} %get-tuple-element.17), channel_id=1, replica_groups=mesh['section_00'=2,'section_01'=2,'section_1'=2,'dom_00'=2,'dom_01'=2,'..., dimensions={0} | all-to-all | bytes 655360 | tf_op jit(solution)/shard_map/all_to_all | solution.py:286
  49.7 0.0 copy-done
  49.8 0.0 copy-done.2
  49.8 1.7 %shard_map.99 = (f32[8,256]{1,0:T(8,128)S(1)}, f32[640,128]{1,0:T(8,128)S(1)}) custom-call(s32[96]{0:T(128)S(1)} %get-tuple-element.14.index_in, f32[1]{0:T(128)S(6)} %copy.10.weight_ref, f32[8,2,6,128,128]{4,3,2,1,0:T(8,128)S(1)} %get-tuple-element.15.blocks_ref, f32[640,128]{1,0:T(8,128)S(1)} %bitcast.7, f32[8,256]{1,0:T(8,128)S(1)} %copy-done, ...), custom_call_target="tpu_custom_call" | custom-call | tf_op jit(solution)/shard_map/pallas_call | solution.py:335
  51.4 10.7 %all_to_all.33.pieces_ref = f32[16,40,128]{2,1,0:T(8,128)S(1)} all-to-all(f32[16,40,128]{2,1,0:T(8,128)S(1)} %bitcast.8), channel_id=1, replica_groups=mesh['section_00'=2,'section_01'=2,'section_1'=2,'dom_00'=2,'dom_01'=2,'..., dimensions={0} | all-to-all | bytes 655360 | tf_op jit(solution)/shard_map/all_to_all | solution.py:286
  62.2 10.1 %all_to_all.34.tiles_ref = f32[8,40,128]{2,1,0:T(8,128)S(1)} all-to-all(f32[8,40,128]{2,1,0:T(8,128)S(1)} %shard_map.100), channel_id=1, replica_groups=mesh['section_00'=2,'section_01'=2,'section_1'=2,'dom_00'=2,'dom_01'=2,'..., dimensions={0} | all-to-all | bytes 327680 | tf_op jit(solution)/shard_map/all_to_all | solution.py:286
  72.3 4.6 %collective-permute-start.1 = (f32[16,128]{1,0:T(8,128)S(1)}, f32[16,128]{1,0:T(8,128)S(1)}, u32[]{:S(2)}, u32[]{:S(2)}) collective-permute-start(f32[16,128]{1,0:T(8,128)S(1)} %shard_map.101), channel_id=1, source_target_pairs={{0,32},{32,0},{1,33},{33,1},{2,34},{34,2},{3,35},{35,3},{4,36},{36... | collective-permute-start | bytes 24584 | tf_op jit(solution)/shard_map/ppermute | solution.py:282
  76.9 0.8 collective-permute-done.1.other_ref
  77.7 0.1 shard_map.102
  77.9 11.0 %all_to_all.35 = f32[16,40,128]{2,1,0:T(8,128)S(1)} all-to-all(f32[16,40,128]{2,1,0:T(8,128)S(1)} %get-tuple-element.22), channel_id=1, replica_groups=mesh['section_00'=2,'section_01'=2,'section_1'=2,'dom_00'=2,'dom_01'=2,'..., dimensions={0} | all-to-all | bytes 655360 | tf_op jit(solution)/shard_map/all_to_all | solution.py:286
  88.9 1.7 %shard_map.103 = (f32[8,256]{1,0:T(8,128)}, f32[8,256]{1,0:T(8,128)}) custom-call(s32[96]{0:T(128)S(1)} %get-tuple-element.14.index_in, f32[8,2,6,128,128]{4,3,2,1,0:T(8,128)S(1)} %get-tuple-element.15.blocks_ref, f32[640,128]{1,0:T(8,128)S(1)} %bitcast.6, f32[8,128]{1,0:T(8,128)S(1)} %get-tuple-element.23.steps_ref, ...), custom_call_target="tpu_custom_call" | custom-call | tf_op jit(solution)/shard_map/pallas_call | solution.py:350
  (5 shorter events, 0.1 us)
Async XLA Ops:
  0.6 49.1 %copy-start = (f32[8,256]{1,0:T(8,128)S(1)}, f32[8,256]{1,0:T(8,128)}, u32[]{:S(2)}) copy-start(f32[8,256]{1,0:T(8,128)} %dual_ref.1) | copy-start | bytes 24580
  0.6 18.4 %copy-start.1 = (f32[8,256]{1,0:T(8,128)S(1)}, f32[8,256]{1,0:T(8,128)}, u32[]{:S(2)}) copy-start(f32[8,256]{1,0:T(8,128)} %cost_ref.3) | copy-start | bytes 24580
  0.7 18.4 %copy-start.3 = (f32[8,256]{1,0:T(8,128)S(1)}, f32[8,256]{1,0:T(8,128)}, u32[]{:S(2)}) copy-start(f32[8,256]{1,0:T(8,128)} %primal_ref.1) | copy-start | bytes 24580
  0.7 49.1 %copy-start.2 = (f32[8,256]{1,0:T(8,128)S(1)}, f32[8,256]{1,0:T(8,128)}, u32[]{:S(2)}) copy-start(f32[8,256]{1,0:T(8,128)} %demand_ref.3) | copy-start | bytes 24580
  34.1 4.6 %collective-permute-start = (f32[16,128]{1,0:T(8,128)S(1)}, f32[16,128]{1,0:T(8,128)S(1)}, u32[]{:S(2)}, u32[]{:S(2)}) collective-permute-start(f32[16,128]{1,0:T(8,128)S(1)} %shard_map.97), channel_id=1, source_target_pairs={{0,32},{32,0},{1,33},{33,1},{2,34},{34,2},{3,35},{35,3},{4,36},{36... | collective-permute-start | bytes 24584 | tf_op jit(solution)/shard_map/ppermute | solution.py:282
  72.3 5.5 %collective-permute-start.1 = (f32[16,128]{1,0:T(8,128)S(1)}, f32[16,128]{1,0:T(8,128)S(1)}, u32[]{:S(2)}, u32[]{:S(2)}) collective-permute-start(f32[16,128]{1,0:T(8,128)S(1)} %shard_map.101), channel_id=1, source_target_pairs={{0,32},{32,0},{1,33},{33,1},{2,34},{34,2},{3,35},{35,3},{4,36},{36... | collective-permute-start | bytes 24584 | tf_op jit(solution)/shard_map/ppermute | solution.py:282
